TPU v7x, 256 devices: a whole 4x4x8 slice. The times are simulated.
256 devices in a mesh: gx: 4 (over z_hi, core), gy: 4 (over z_lo), gz: 16 (over y, x).
Axes of the slice: x: 4, y: 4, z: 8 (z_hi: 2, z_lo: 4; z = z_hi * 4 + z_lo), core: 2. Of those that a mesh axis runs over, the one named last changes fastest.
Arguments:
- observed: float32 [512, 128, 512], P('gz', 'gx', 'gy'), may hold values from 0.25 to 4
- profile_x: float32 [31], replicated, may hold values from 0.05 to 1
- profile_y: float32 [31], replicated, may hold values from 0.05 to 1
- profile_z: float32 [61], replicated, may hold values from 0.05 to 1
Outputs:
- estimate: float32 [512, 128, 512], P('gz', 'gx', 'gy')
- level_two: float32 [64, 256, 256], P('gx', ('gy', 'gz'))
- level_four: float32 [32, 128, 128], P('gx', ('gy', 'gz'))
- level_eight: float32 [16, 64, 64], P('gx', ('gy', 'gz'))
All inputs are finite; a program needn't handle non-finite values.
Results may differ from a plain program's by a relative error of at most 0.0001.
Values sent between devices are 32-bit elements; how exact they have to be, the bound alone decides.
A program may use at most 128 MiB of HBM per device.

v0:
```python
import jax
import jax.numpy as jnp
from jax import lax
from jax.sharding import PartitionSpec as P

TAPS_X = 31
TAPS_Y = 31
TAPS_Z = 61
ITERS = 2


def extended_2(value, sides, width):
    for axis, dim in sides:
        devices, length = (lax.axis_size(axis), value.shape[dim])
        up = [(i, (i + 1) % devices) for i in range(devices - 1)]
        down = [(j, i) for i, j in up]
        last = lax.slice_in_dim(value, length - width, length, axis=dim)
        initial = lax.slice_in_dim(value, 0, width, axis=dim)
        before = lax.ppermute(last, axis, up)
        after = lax.ppermute(initial, axis, down)
        value = jnp.concatenate([before, value, after], axis=dim)
    return value


def band_matrix(kernel, row_count, col_count, offset, adjoint):
    tap_count = kernel.shape[0]
    half = (tap_count - 1) // 2
    rowsidx = jnp.arange(row_count)[:, None]
    colsidx = jnp.arange(col_count)[None, :]
    if adjoint:
        which = colsidx + half + offset - rowsidx
    else:
        which = rowsidx - offset - colsidx + half
    inside = (which >= 0) & (which < tap_count)
    picked = kernel[jnp.clip(which, 0, tap_count - 1)]
    return jnp.where(inside, picked, 0.0)


def along_x(field, kernel, adjoint):
    half = (TAPS_X - 1) // 2
    extended = extended_2(field, (("gx", 1),), half)
    matrix = band_matrix(kernel, extended.shape[1], field.shape[1], half, adjoint)
    return jnp.einsum("zry,rc->zcy", extended, matrix, precision=lax.Precision.HIGHEST)


def along_y(field, kernel, adjoint):
    half = (TAPS_Y - 1) // 2
    extended = extended_2(field, (("gy", 2),), half)
    matrix = band_matrix(kernel, extended.shape[2], field.shape[2], half, adjoint)
    return jnp.einsum("zxr,rc->zxc", extended, matrix, precision=lax.Precision.HIGHEST)


def along_z(field, kernel, adjoint):
    half = (TAPS_Z - 1) // 2
    depth = field.shape[0]
    extended = extended_2(field, (("gz", 0),), half)
    matrix = band_matrix(kernel, extended.shape[0], depth, half, adjoint)
    return jnp.einsum("rxy,rc->cxy", extended, matrix, precision=lax.Precision.HIGHEST)


def pool_half(field):
    sx, sy, sz = field.shape
    return field.reshape(sx // 2, 2, sy // 2, 2, sz // 2, 2).mean(axis=(1, 3, 5))


def shards(observed, profile_x, profile_y, profile_z):
    kernel_x = profile_x / jnp.sum(profile_x)
    kernel_y = profile_y / jnp.sum(profile_y)
    kernel_z = profile_z / jnp.sum(profile_z)
    estimate = observed
    for step in range(ITERS):
        blurred = along_x(estimate, kernel_x, False)
        blurred = along_y(blurred, kernel_y, False)
        blurred = along_z(blurred, kernel_z, False)
        ratio = observed / blurred
        correction = along_z(ratio, kernel_z, True)
        correction = along_y(correction, kernel_y, True)
        correction = along_x(correction, kernel_x, True)
        estimate = estimate * correction
    relaid = lax.all_to_all(estimate, "gz", split_axis=2, concat_axis=0, tiled=True)
    level_two = pool_half(jnp.transpose(relaid, (1, 2, 0)))
    level_four = pool_half(level_two)
    level_eight = pool_half(level_four)
    return (estimate, level_two, level_four, level_eight)


def solution(mesh):
    placed = (P("gz", "gx", "gy"), P(), P(), P())
    return jax.shard_map(
        shards,
        mesh=mesh,
        in_specs=placed,
        out_specs=(
            P("gz", "gx", "gy"),
            P("gx", ("gy", "gz"), None),
            P("gx", ("gy", "gz"), None),
            P("gx", ("gy", "gz"), None),
        ),
        check_vma=False,
    )
```

profile of v0, /device:TPU:1, one launch (start us, length us, event | category | flops | bytes accessed | tf_op | source)
XLA Modules:
  0.0 411.6 jit_solution(6876161370571932406)
XLA Ops:
  1.7 10.2 %collective-permute-start = (f32[32,15,128]{2,1,0:T(8,128)S(1)}, f32[32,15,128]{2,1,0:T(8,128)S(1)}, u32[]{:S(2)}, u32[]{:S(2)}) collective-permute-start(f32[32,15,128]{2,1,0:T(8,128)S(1)} %get-tuple-element.30), channel_id=1, source_target_pairs={{0,64},{64,128},{128,192},{1,65},{65,129},{129,193},{2,66},{66,130... | collective-permute-start | bytes 737288 | tf_op jit(solution)/shard_map/ppermute | solution.py:19
  11.9 1.9 collective-permute-start.1
  13.9 1.3 reduce_sum.63
  15.1 1.3 broadcast_divide_fusion
  16.4 1.3 reduce_sum.61
  17.7 1.3 broadcast_divide_fusion.2
  19.2 1.2 reduce_sum.62
  20.4 12.3 %gather_fusion.3 = f32[1984]{0:T(1024)S(1)} fusion(f32[31]{0:T(128)S(1)} %broadcast_divide_fusion.2, s32[2048]{0:T(1024)S(1)} %pad_clamp_fusion.2), kind=kCustom, calls=%fused_computation.3 | custom fusion | bytes 23808 | tf_op jit(solution)/shard_map/gather | solution.py:35
  35.2 2.7 collective-permute-start.2
  37.9 1.3 collective-permute-start.3
  39.2 4.8 %collective-permute-done.2 = f32[32,32,15]{2,1,0:T(8,128)S(1)} collective-permute-done((f32[32,32,15]{2,1,0:T(8,128)S(1)}, f32[32,32,15]{2,1,0:T(8,128)S(1)}, u32[]{:S(2)}, u32[]{:S(2)}) %collective-permute-start.2) | collective-permute-done | bytes 61472 | tf_op jit(solution)/shard_map/ppermute | solution.py:19
  44.0 3.8 collective-permute-done.3
  47.9 20.9 %fusion.29 = f32[32,32,128]{2,1,0:T(8,128)S(1)} fusion(f32[32,32,15]{2,1,0:T(8,128)S(1)} %collective-permute-done.3, f32[32,32,128]{2,1,0:T(8,128)S(1)} %convolution_bitcast_fusion.3, f32[32,32,15]{2,1,0:T(8,128)S(1)} %collective-permute-done.2, f32[]{:T(128)} %bitcast.53, f32[]{:T(128)} %bitcast.54, f32[]{:T(128)} %bitcast.55, f32[]{:T(128)} %bitcast.56, ...), kind=kOutput, calls=%fused_computation.35 | convolution fusion | flops 250292224 | bytes 1172212 | tf_op jit(solution)/shard_map/zxr,rc->zxc/dot_general | solution.py:50
  68.9 3.1 collective-permute-start.4
  72.0 1.3 collective-permute-start.5
  74.1 16.9 %gather_fusion.2 = f32[2944]{0:T(1024)S(1)} fusion(f32[61]{0:T(128)S(1)} %broadcast_divide_fusion.1, s32[3072]{0:T(1024)S(1)} %pad_clamp_fusion), kind=kCustom, calls=%fused_computation.2 | custom fusion | bytes 35328 | tf_op jit(solution)/shard_map/gather | solution.py:35
  91.2 2.0 fusion.16
  93.3 4.0 collective-permute-start.6
  97.3 1.3 collective-permute-start.7
  98.8 16.9 %gather_fusion.1 = f32[2944]{0:T(1024)S(1)} fusion(f32[61]{0:T(128)S(1)} %broadcast_divide_fusion.1, s32[3072]{0:T(1024)S(1)} %pad_clamp_fusion.1), kind=kCustom, calls=%fused_computation.1 | custom fusion | bytes 35328 | tf_op jit(solution)/shard_map/gather | solution.py:35
  117.0 3.2 collective-permute-start.8
  120.2 1.3 collective-permute-start.9
  121.5 7.3 %collective-permute-done.8 = f32[32,32,15]{2,0,1:T(8,128)S(1)} collective-permute-done((f32[32,32,15]{2,0,1:T(8,128)S(1)}, f32[32,32,15]{2,0,1:T(8,128)S(1)}, u32[]{:S(2)}, u32[]{:S(2)}) %collective-permute-start.8) | collective-permute-done | bytes 61472 | tf_op jit(solution)/shard_map/ppermute | solution.py:19
  128.8 4.9 %collective-permute-done.9 = f32[32,32,15]{2,0,1:T(8,128)S(1)} collective-permute-done((f32[32,32,15]{2,0,1:T(8,128)S(1)}, f32[32,32,15]{2,0,1:T(8,128)S(1)}, u32[]{:S(2)}, u32[]{:S(2)}) %collective-permute-start.9) | collective-permute-done | bytes 61472 | tf_op jit(solution)/shard_map/ppermute | solution.py:20
  134.2 21.2 %fusion.58 = f32[32,32,128]{2,1,0:T(8,128)S(1)} fusion(f32[32,32,158]{2,0,1:T(8,128)S(1)} %pad_maximum_fusion.2, f32[]{:T(128)} %bitcast.53, f32[]{:T(128)} %bitcast.54, f32[]{:T(128)} %bitcast.55, f32[]{:T(128)} %bitcast.56, f32[]{:T(128)} %bitcast.57, f32[]{:T(128)} %bitcast.59, f32[]{:T(128)} %bitcast.58, f32[]{:T(128)} %bitcast.6, f32[]{:T(128)} %bitcast.8, ...), kind=kOutput, calls=%fused_computation.66 | convolution fusion | flops 249928192 | bytes 1172092 | tf_op jit(solution)/shard_map/zxr,rc->zxc/dot_general | solution.py:50
  155.4 7.1 %collective-permute-start.10 = (f32[32,15,128]{2,1,0:T(8,128)S(1)}, f32[32,15,128]{2,1,0:T(8,128)S(1)}, u32[]{:S(2)}, u32[]{:S(2)}) collective-permute-start(f32[32,15,128]{2,1,0:T(8,128)S(1)} %get-tuple-element.20), channel_id=1, source_target_pairs={{0,64},{64,128},{128,192},{1,65},{65,129},{129,193},{2,66},{66,130... | collective-permute-start | bytes 737288 | tf_op jit(solution)/shard_map/ppermute | solution.py:19
  162.5 2.1 collective-permute-start.11
  164.8 12.3 %gather_fusion = f32[1984]{0:T(1024)S(1)} fusion(f32[31]{0:T(128)S(1)} %broadcast_divide_fusion.2, s32[2048]{0:T(1024)S(1)} %pad_clamp_fusion.3), kind=kCustom, calls=%fused_computation | custom fusion | bytes 23808 | tf_op jit(solution)/shard_map/gather | solution.py:35
  177.9 7.5 %collective-permute-start.12 = (f32[32,15,128]{2,1,0:T(8,128)S(1)}, f32[32,15,128]{2,1,0:T(8,128)S(1)}, u32[]{:S(2)}, u32[]{:S(2)}) collective-permute-start(f32[32,15,128]{2,1,0:T(8,128)S(1)} %get-tuple-element.18), channel_id=1, source_target_pairs={{0,64},{64,128},{128,192},{1,65},{65,129},{129,193},{2,66},{66,130... | collective-permute-start | bytes 737288 | tf_op jit(solution)/shard_map/ppermute | solution.py:19
  185.5 1.9 collective-permute-start.13
  187.4 1.4 collective-permute-done.12
  188.8 11.9 %collective-permute-done.13 = f32[32,15,128]{2,1,0:T(8,128)S(1)} collective-permute-done((f32[32,15,128]{2,1,0:T(8,128)S(1)}, f32[32,15,128]{2,1,0:T(8,128)S(1)}, u32[]{:S(2)}, u32[]{:S(2)}) %collective-permute-start.13) | collective-permute-done | bytes 245792 | tf_op jit(solution)/shard_map/ppermute | solution.py:20
  201.7 2.8 collective-permute-start.14
  204.5 1.3 collective-permute-start.15
  205.8 4.8 %collective-permute-done.14 = f32[32,32,15]{2,1,0:T(8,128)S(1)} collective-permute-done((f32[32,32,15]{2,1,0:T(8,128)S(1)}, f32[32,32,15]{2,1,0:T(8,128)S(1)}, u32[]{:S(2)}, u32[]{:S(2)}) %collective-permute-start.14) | collective-permute-done | bytes 61472 | tf_op jit(solution)/shard_map/ppermute | solution.py:19
  210.6 4.0 collective-permute-done.15
  214.6 20.9 %fusion.45 = f32[32,32,128]{2,1,0:T(8,128)S(1)} fusion(f32[32,32,15]{2,1,0:T(8,128)S(1)} %collective-permute-done.15, f32[32,32,128]{2,1,0:T(8,128)S(1)} %convolution_bitcast_fusion.1, f32[32,32,15]{2,1,0:T(8,128)S(1)} %collective-permute-done.14, f32[]{:T(128)} %bitcast.53, f32[]{:T(128)} %bitcast.54, f32[]{:T(128)} %bitcast.55, f32[]{:T(128)} %bitcast.56, ...), kind=kOutput, calls=%fused_computation.52 | convolution fusion | flops 250292224 | bytes 1172212 | tf_op jit(solution)/shard_map/zxr,rc->zxc/dot_general | solution.py:50
  235.6 4.3 %collective-permute-start.16 = (f32[30,32,128]{2,1,0:T(8,128)S(1)}, f32[30,32,128]{2,1,0:T(8,128)S(1)}, u32[]{:S(2)}, u32[]{:S(2)}) collective-permute-start(f32[30,32,128]{2,1,0:T(8,128)S(1)} %get-tuple-element.14), channel_id=1, source_target_pairs={{0,1},{1,2},{2,3},{3,4},{4,5},{5,6},{6,7},{7,8},{8,9},{9,10},{10,1... | collective-permute-start | bytes 1474568 | tf_op jit(solution)/shard_map/ppermute | solution.py:19
  239.9 1.3 collective-permute-start.17
  241.2 4.4 %collective-permute-done.16 = f32[30,32,128]{2,1,0:T(8,128)S(1)} collective-permute-done((f32[30,32,128]{2,1,0:T(8,128)S(1)}, f32[30,32,128]{2,1,0:T(8,128)S(1)}, u32[]{:S(2)}, u32[]{:S(2)}) %collective-permute-start.16) | collective-permute-done | bytes 491552 | tf_op jit(solution)/shard_map/ppermute | solution.py:19
  245.6 3.8 collective-permute-done.17
  249.6 2.0 fusion.19
  251.7 4.4 %collective-permute-start.18 = (f32[30,32,128]{2,0,1:T(8,128)S(1)}, f32[30,32,128]{2,0,1:T(8,128)S(1)}, u32[]{:S(2)}, u32[]{:S(2)}) collective-permute-start(f32[30,32,128]{2,0,1:T(8,128)S(1)} %get-tuple-element.12), channel_id=1, source_target_pairs={{0,1},{1,2},{2,3},{3,4},{4,5},{5,6},{6,7},{7,8},{8,9},{9,10},{10,1... | collective-permute-start | bytes 1474568 | tf_op jit(solution)/shard_map/ppermute | solution.py:19
  256.2 1.3 collective-permute-start.19
  257.5 4.8 %collective-permute-done.18 = f32[30,32,128]{2,0,1:T(8,128)S(1)} collective-permute-done((f32[30,32,128]{2,0,1:T(8,128)S(1)}, f32[30,32,128]{2,0,1:T(8,128)S(1)}, u32[]{:S(2)}, u32[]{:S(2)}) %collective-permute-start.18) | collective-permute-done | bytes 491552 | tf_op jit(solution)/shard_map/ppermute | solution.py:19
  262.2 6.2 %collective-permute-done.19 = f32[30,32,128]{2,0,1:T(8,128)S(1)} collective-permute-done((f32[30,32,128]{2,0,1:T(8,128)S(1)}, f32[30,32,128]{2,0,1:T(8,128)S(1)}, u32[]{:S(2)}, u32[]{:S(2)}) %collective-permute-start.19) | collective-permute-done | bytes 491552 | tf_op jit(solution)/shard_map/ppermute | solution.py:20
  269.7 3.7 collective-permute-start.20
  273.4 1.3 collective-permute-start.21
  274.7 4.8 %collective-permute-done.20 = f32[32,32,15]{2,0,1:T(8,128)S(1)} collective-permute-done((f32[32,32,15]{2,0,1:T(8,128)S(1)}, f32[32,32,15]{2,0,1:T(8,128)S(1)}, u32[]{:S(2)}, u32[]{:S(2)}) %collective-permute-start.20) | collective-permute-done | bytes 61472 | tf_op jit(solution)/shard_map/ppermute | solution.py:19
  279.4 3.8 collective-permute-done.21
  283.8 21.2 %fusion.56 = f32[32,32,128]{2,1,0:T(8,128)S(1)} fusion(f32[32,32,158]{2,0,1:T(8,128)S(1)} %pad_maximum_fusion.3, f32[]{:T(128)} %bitcast.53, f32[]{:T(128)} %bitcast.54, f32[]{:T(128)} %bitcast.55, f32[]{:T(128)} %bitcast.56, f32[]{:T(128)} %bitcast.57, f32[]{:T(128)} %bitcast.59, f32[]{:T(128)} %bitcast.58, f32[]{:T(128)} %bitcast.6, f32[]{:T(128)} %bitcast.8, ...), kind=kOutput, calls=%fused_computation.64 | convolution fusion | flops 249928192 | bytes 1172092 | tf_op jit(solution)/shard_map/zxr,rc->zxc/dot_general | solution.py:50
  305.0 6.0 %collective-permute-start.22 = (f32[32,15,128]{2,1,0:T(8,128)S(1)}, f32[32,15,128]{2,1,0:T(8,128)S(1)}, u32[]{:S(2)}, u32[]{:S(2)}) collective-permute-start(f32[32,15,128]{2,1,0:T(8,128)S(1)} %get-tuple-element.8), channel_id=1, source_target_pairs={{0,64},{64,128},{128,192},{1,65},{65,129},{129,193},{2,66},{66,130... | collective-permute-start | bytes 737288 | tf_op jit(solution)/shard_map/ppermute | solution.py:19
  311.0 2.1 collective-permute-start.23
  313.2 1.1 collective-permute-done.22
  314.3 8.3 %collective-permute-done.23 = f32[32,15,128]{2,1,0:T(8,128)S(1)} collective-permute-done((f32[32,15,128]{2,1,0:T(8,128)S(1)}, f32[32,15,128]{2,1,0:T(8,128)S(1)}, u32[]{:S(2)}, u32[]{:S(2)}) %collective-permute-start.23) | collective-permute-done | bytes 245792 | tf_op jit(solution)/shard_map/ppermute | solution.py:20
  323.4 1.8 copy.45
  326.1 20.7 %all_to_all.18 = f32[16,1,8192]{2,1,0:T(1,128)S(1)} all-to-all(f32[16,1,8192]{2,1,0:T(1,128)S(1)} %reshape.596), channel_id=1, replica_groups=mesh['gx'=4,'gy'=4,'gz'=16] {'gz'}, dimensions={0} | all-to-all | bytes 1048576 | tf_op jit(solution)/shard_map/all_to_all | solution.py:80
  347.4 1.9 reduce.3
  349.9 2.7 copy.47
  352.6 2.3 all_to_all.16
  354.9 34.8 %reshape.317 = f32[16,2,4,2,256,2]{5,4,3,2,1,0:T(8,128)} reshape(f32[32,8,512]{2,1,0:T(8,128)S(1)} %bitcast.676) | data formatting | bytes 1048576 | tf_op jit(solution)/shard_map/reshape | solution.py:63
  389.8 12.2 %reduce_sum.64 = f32[16,4,256]{2,1,0:T(4,128)S(1)} reduce(f32[16,2,4,2,256,2]{5,4,3,2,1,0:T(8,128)} %reshape.317, f32[]{:T(128)} %constant.13.clone.1), dimensions={1,3,5}, to_apply=%region_3.4 | reduce | flops 114688 | bytes 589828 | tf_op jit(solution)/shard_map/reduce_sum | solution.py:63
  402.0 5.5 %div.56 = f32[8,2,2,2,128,2]{5,4,1,0,3,2:T(8,128)} reshape(f32[16,4,256]{2,0,1:T(8,128)S(1)} %copy.48) | data formatting | bytes 131072 | tf_op jit(solution)/shard_map/div | solution.py:63
  407.6 2.5 reduce_sum.65
  (73 shorter events, 15.2 us)
Async XLA Ops:
  1.7 32.5 %collective-permute-start = (f32[32,15,128]{2,1,0:T(8,128)S(1)}, f32[32,15,128]{2,1,0:T(8,128)S(1)}, u32[]{:S(2)}, u32[]{:S(2)}) collective-permute-start(f32[32,15,128]{2,1,0:T(8,128)S(1)} %get-tuple-element.30), channel_id=1, source_target_pairs={{0,64},{64,128},{128,192},{1,65},{65,129},{129,193},{2,66},{66,130... | collective-permute-start | bytes 737288 | tf_op jit(solution)/shard_map/ppermute | solution.py:19
  11.9 22.3 %collective-permute-start.1 = (f32[32,15,128]{2,1,0:T(8,128)S(1)}, f32[32,15,128]{2,1,0:T(8,128)S(1)}, u32[]{:S(2)}, u32[]{:S(2)}) collective-permute-start(f32[32,15,128]{2,1,0:T(8,128)S(1)} %get-tuple-element.31), channel_id=1, source_target_pairs={{64,0},{128,64},{192,128},{65,1},{129,65},{193,129},{66,2},{130,66... | collective-permute-start | bytes 737288 | tf_op jit(solution)/shard_map/ppermute | solution.py:20
  20.4 13.8 %copy-start = (f32[32,32,128]{2,1,0:T(8,128)S(1)}, f32[32,32,128]{2,1,0:T(8,128)}, u32[]{:S(2)}) copy-start(f32[32,32,128]{2,1,0:T(8,128)} %param.4) | copy-start | bytes 1572868
  35.2 8.8 %collective-permute-start.2 = (f32[32,32,15]{2,1,0:T(8,128)S(1)}, f32[32,32,15]{2,1,0:T(8,128)S(1)}, u32[]{:S(2)}, u32[]{:S(2)}) collective-permute-start(f32[32,32,15]{2,1,0:T(8,128)S(1)} %get-tuple-element.28), channel_id=1, source_target_pairs={{0,16},{16,32},{32,48},{1,17},{17,33},{33,49},{2,18},{18,34},{34,5... | collective-permute-start | bytes 184328 | tf_op jit(solution)/shard_map/ppermute | solution.py:19
  37.9 9.9 %collective-permute-start.3 = (f32[32,32,15]{2,1,0:T(8,128)S(1)}, f32[32,32,15]{2,1,0:T(8,128)S(1)}, u32[]{:S(2)}, u32[]{:S(2)}) collective-permute-start(f32[32,32,15]{2,1,0:T(8,128)S(1)} %get-tuple-element.29), channel_id=1, source_target_pairs={{16,0},{32,16},{48,32},{17,1},{33,17},{49,33},{18,2},{34,18},{50,3... | collective-permute-start | bytes 184328 | tf_op jit(solution)/shard_map/ppermute | solution.py:20
  68.8 4.8 %copy-start.3 = (f32[61]{0:T(128)S(1)}, f32[61]{0:T(128)}, u32[]{:S(2)}) copy-start(f32[61]{0:T(128)} %param.7) | copy-start | bytes 736
  68.9 22.2 %collective-permute-start.4 = (f32[30,32,128]{2,1,0:T(8,128)S(1)}, f32[30,32,128]{2,1,0:T(8,128)S(1)}, u32[]{:S(2)}, u32[]{:S(2)}) collective-permute-start(f32[30,32,128]{2,1,0:T(8,128)S(1)} %get-tuple-element.26), channel_id=1, source_target_pairs={{0,1},{1,2},{2,3},{3,4},{4,5},{5,6},{6,7},{7,8},{8,9},{9,10},{10,1... | collective-permute-start | bytes 1474568 | tf_op jit(solution)/shard_map/ppermute | solution.py:19
  72.0 19.0 %collective-permute-start.5 = (f32[30,32,128]{2,1,0:T(8,128)S(1)}, f32[30,32,128]{2,1,0:T(8,128)S(1)}, u32[]{:S(2)}, u32[]{:S(2)}) collective-permute-start(f32[30,32,128]{2,1,0:T(8,128)S(1)} %get-tuple-element.27), channel_id=1, source_target_pairs={{1,0},{2,1},{3,2},{4,3},{5,4},{6,5},{7,6},{8,7},{9,8},{10,9},{11,1... | collective-permute-start | bytes 1474568 | tf_op jit(solution)/shard_map/ppermute | solution.py:20
  93.3 22.4 %collective-permute-start.6 = (f32[30,32,128]{2,0,1:T(8,128)S(1)}, f32[30,32,128]{2,0,1:T(8,128)S(1)}, u32[]{:S(2)}, u32[]{:S(2)}) collective-permute-start(f32[30,32,128]{2,0,1:T(8,128)S(1)} %get-tuple-element.24), channel_id=1, source_target_pairs={{0,1},{1,2},{2,3},{3,4},{4,5},{5,6},{6,7},{7,8},{8,9},{9,10},{10,1... | collective-permute-start | bytes 1474568 | tf_op jit(solution)/shard_map/ppermute | solution.py:19
  97.3 18.4 %collective-permute-start.7 = (f32[30,32,128]{2,0,1:T(8,128)S(1)}, f32[30,32,128]{2,0,1:T(8,128)S(1)}, u32[]{:S(2)}, u32[]{:S(2)}) collective-permute-start(f32[30,32,128]{2,0,1:T(8,128)S(1)} %get-tuple-element.25), channel_id=1, source_target_pairs={{1,0},{2,1},{3,2},{4,3},{5,4},{6,5},{7,6},{8,7},{9,8},{10,9},{11,1... | collective-permute-start | bytes 1474568 | tf_op jit(solution)/shard_map/ppermute | solution.py:20
  117.0 11.8 %collective-permute-start.8 = (f32[32,32,15]{2,0,1:T(8,128)S(1)}, f32[32,32,15]{2,0,1:T(8,128)S(1)}, u32[]{:S(2)}, u32[]{:S(2)}) collective-permute-start(f32[32,32,15]{2,0,1:T(8,128)S(1)} %get-tuple-element.22), channel_id=1, source_target_pairs={{0,16},{16,32},{32,48},{1,17},{17,33},{33,49},{2,18},{18,34},{34,5... | collective-permute-start | bytes 184328 | tf_op jit(solution)/shard_map/ppermute | solution.py:19
  120.2 13.5 %collective-permute-start.9 = (f32[32,32,15]{2,0,1:T(8,128)S(1)}, f32[32,32,15]{2,0,1:T(8,128)S(1)}, u32[]{:S(2)}, u32[]{:S(2)}) collective-permute-start(f32[32,32,15]{2,0,1:T(8,128)S(1)} %get-tuple-element.23), channel_id=1, source_target_pairs={{16,0},{32,16},{48,32},{17,1},{33,17},{49,33},{18,2},{34,18},{50,3... | collective-permute-start | bytes 184328 | tf_op jit(solution)/shard_map/ppermute | solution.py:20
  155.4 21.7 %collective-permute-start.10 = (f32[32,15,128]{2,1,0:T(8,128)S(1)}, f32[32,15,128]{2,1,0:T(8,128)S(1)}, u32[]{:S(2)}, u32[]{:S(2)}) collective-permute-start(f32[32,15,128]{2,1,0:T(8,128)S(1)} %get-tuple-element.20), channel_id=1, source_target_pairs={{0,64},{64,128},{128,192},{1,65},{65,129},{129,193},{2,66},{66,130... | collective-permute-start | bytes 737288 | tf_op jit(solution)/shard_map/ppermute | solution.py:19
  162.5 14.6 %collective-permute-start.11 = (f32[32,15,128]{2,1,0:T(8,128)S(1)}, f32[32,15,128]{2,1,0:T(8,128)S(1)}, u32[]{:S(2)}, u32[]{:S(2)}) collective-permute-start(f32[32,15,128]{2,1,0:T(8,128)S(1)} %get-tuple-element.21), channel_id=1, source_target_pairs={{64,0},{128,64},{192,128},{65,1},{129,65},{193,129},{66,2},{130,66... | collective-permute-start | bytes 737288 | tf_op jit(solution)/shard_map/ppermute | solution.py:20
  177.9 10.9 %collective-permute-start.12 = (f32[32,15,128]{2,1,0:T(8,128)S(1)}, f32[32,15,128]{2,1,0:T(8,128)S(1)}, u32[]{:S(2)}, u32[]{:S(2)}) collective-permute-start(f32[32,15,128]{2,1,0:T(8,128)S(1)} %get-tuple-element.18), channel_id=1, source_target_pairs={{0,64},{64,128},{128,192},{1,65},{65,129},{129,193},{2,66},{66,130... | collective-permute-start | bytes 737288 | tf_op jit(solution)/shard_map/ppermute | solution.py:19
  185.5 15.2 %collective-permute-start.13 = (f32[32,15,128]{2,1,0:T(8,128)S(1)}, f32[32,15,128]{2,1,0:T(8,128)S(1)}, u32[]{:S(2)}, u32[]{:S(2)}) collective-permute-start(f32[32,15,128]{2,1,0:T(8,128)S(1)} %get-tuple-element.19), channel_id=1, source_target_pairs={{64,0},{128,64},{192,128},{65,1},{129,65},{193,129},{66,2},{130,66... | collective-permute-start | bytes 737288 | tf_op jit(solution)/shard_map/ppermute | solution.py:20
  201.7 8.9 %collective-permute-start.14 = (f32[32,32,15]{2,1,0:T(8,128)S(1)}, f32[32,32,15]{2,1,0:T(8,128)S(1)}, u32[]{:S(2)}, u32[]{:S(2)}) collective-permute-start(f32[32,32,15]{2,1,0:T(8,128)S(1)} %get-tuple-element.16), channel_id=1, source_target_pairs={{0,16},{16,32},{32,48},{1,17},{17,33},{33,49},{2,18},{18,34},{34,5... | collective-permute-start | bytes 184328 | tf_op jit(solution)/shard_map/ppermute | solution.py:19
  204.5 10.1 %collective-permute-start.15 = (f32[32,32,15]{2,1,0:T(8,128)S(1)}, f32[32,32,15]{2,1,0:T(8,128)S(1)}, u32[]{:S(2)}, u32[]{:S(2)}) collective-permute-start(f32[32,32,15]{2,1,0:T(8,128)S(1)} %get-tuple-element.17), channel_id=1, source_target_pairs={{16,0},{32,16},{48,32},{17,1},{33,17},{49,33},{18,2},{34,18},{50,3... | collective-permute-start | bytes 184328 | tf_op jit(solution)/shard_map/ppermute | solution.py:20
  235.6 10.0 %collective-permute-start.16 = (f32[30,32,128]{2,1,0:T(8,128)S(1)}, f32[30,32,128]{2,1,0:T(8,128)S(1)}, u32[]{:S(2)}, u32[]{:S(2)}) collective-permute-start(f32[30,32,128]{2,1,0:T(8,128)S(1)} %get-tuple-element.14), channel_id=1, source_target_pairs={{0,1},{1,2},{2,3},{3,4},{4,5},{5,6},{6,7},{7,8},{8,9},{9,10},{10,1... | collective-permute-start | bytes 1474568 | tf_op jit(solution)/shard_map/ppermute | solution.py:19
  239.9 9.6 %collective-permute-start.17 = (f32[30,32,128]{2,1,0:T(8,128)S(1)}, f32[30,32,128]{2,1,0:T(8,128)S(1)}, u32[]{:S(2)}, u32[]{:S(2)}) collective-permute-start(f32[30,32,128]{2,1,0:T(8,128)S(1)} %get-tuple-element.15), channel_id=1, source_target_pairs={{1,0},{2,1},{3,2},{4,3},{5,4},{6,5},{7,6},{8,7},{9,8},{10,9},{11,1... | collective-permute-start | bytes 1474568 | tf_op jit(solution)/shard_map/ppermute | solution.py:20
  251.7 10.5 %collective-permute-start.18 = (f32[30,32,128]{2,0,1:T(8,128)S(1)}, f32[30,32,128]{2,0,1:T(8,128)S(1)}, u32[]{:S(2)}, u32[]{:S(2)}) collective-permute-start(f32[30,32,128]{2,0,1:T(8,128)S(1)} %get-tuple-element.12), channel_id=1, source_target_pairs={{0,1},{1,2},{2,3},{3,4},{4,5},{5,6},{6,7},{7,8},{8,9},{9,10},{10,1... | collective-permute-start | bytes 1474568 | tf_op jit(solution)/shard_map/ppermute | solution.py:19
  256.2 12.3 %collective-permute-start.19 = (f32[30,32,128]{2,0,1:T(8,128)S(1)}, f32[30,32,128]{2,0,1:T(8,128)S(1)}, u32[]{:S(2)}, u32[]{:S(2)}) collective-permute-start(f32[30,32,128]{2,0,1:T(8,128)S(1)} %get-tuple-element.13), channel_id=1, source_target_pairs={{1,0},{2,1},{3,2},{4,3},{5,4},{6,5},{7,6},{8,7},{9,8},{10,9},{11,1... | collective-permute-start | bytes 1474568 | tf_op jit(solution)/shard_map/ppermute | solution.py:20
  269.7 9.8 %collective-permute-start.20 = (f32[32,32,15]{2,0,1:T(8,128)S(1)}, f32[32,32,15]{2,0,1:T(8,128)S(1)}, u32[]{:S(2)}, u32[]{:S(2)}) collective-permute-start(f32[32,32,15]{2,0,1:T(8,128)S(1)} %get-tuple-element.10), channel_id=1, source_target_pairs={{0,16},{16,32},{32,48},{1,17},{17,33},{33,49},{2,18},{18,34},{34,5... | collective-permute-start | bytes 184328 | tf_op jit(solution)/shard_map/ppermute | solution.py:19
  273.4 9.9 %collective-permute-start.21 = (f32[32,32,15]{2,0,1:T(8,128)S(1)}, f32[32,32,15]{2,0,1:T(8,128)S(1)}, u32[]{:S(2)}, u32[]{:S(2)}) collective-permute-start(f32[32,32,15]{2,0,1:T(8,128)S(1)} %get-tuple-element.11), channel_id=1, source_target_pairs={{16,0},{32,16},{48,32},{17,1},{33,17},{49,33},{18,2},{34,18},{50,3... | collective-permute-start | bytes 184328 | tf_op jit(solution)/shard_map/ppermute | solution.py:20
  305.0 9.3 %collective-permute-start.22 = (f32[32,15,128]{2,1,0:T(8,128)S(1)}, f32[32,15,128]{2,1,0:T(8,128)S(1)}, u32[]{:S(2)}, u32[]{:S(2)}) collective-permute-start(f32[32,15,128]{2,1,0:T(8,128)S(1)} %get-tuple-element.8), channel_id=1, source_target_pairs={{0,64},{64,128},{128,192},{1,65},{65,129},{129,193},{2,66},{66,130... | collective-permute-start | bytes 737288 | tf_op jit(solution)/shard_map/ppermute | solution.py:19
  311.0 11.6 %collective-permute-start.23 = (f32[32,15,128]{2,1,0:T(8,128)S(1)}, f32[32,15,128]{2,1,0:T(8,128)S(1)}, u32[]{:S(2)}, u32[]{:S(2)}) collective-permute-start(f32[32,15,128]{2,1,0:T(8,128)S(1)} %get-tuple-element.9), channel_id=1, source_target_pairs={{64,0},{128,64},{192,128},{65,1},{129,65},{193,129},{66,2},{130,66... | collective-permute-start | bytes 737288 | tf_op jit(solution)/shard_map/ppermute | solution.py:20
  323.3 2.8 copy-start.1
  402.0 5.6 %copy-start.2 = (f32[16,4,256]{2,1,0:T(4,128)}, f32[16,4,256]{2,1,0:T(4,128)S(1)}, u32[]{:S(2)}) copy-start(f32[16,4,256]{2,1,0:T(4,128)S(1)} %broadcast_multiply_fusion) | copy-start | bytes 196612
where the time goes:
time: 414 us; the launch traced here: 412 us
  local copies, waits for them, and re-layouts  113 us (27%)
  matrix products  93.3 us (23%)
  waiting for transfers between devices  80.1 us (19%)
  starting transfers between devices  77.6 us (19%)
  other arithmetic  25.7 us (6%)
  blocking collectives  20.7 us (5%)
    dot_general x4, matrix products, along_y(): jnp.einsum('zxr,rc->zxc', extended, matrix, precision=lax.Precision.HIGHEST)  84.2 us
    gather x10, local copies, waits for them, and re-layouts, band_matrix(): picked = kernel[jnp.clip(which, 0, tap_count - 1)]  60 us
    ppermute x12, starting transfers between devices, extended_2(): before = lax.ppermute(last, axis, up)  59.1 us
    ppermute x12, waiting for transfers between devices, extended_2(): after = lax.ppermute(initial, axis, down)  46.8 us
    reshape x1, local copies, waits for them, and re-layouts, pool_half(): field.reshape(sx // 2, 2, sy // 2, 2, sz // 2, 2).mean(axis=(1, 3, 5))  34.8 us
    ppermute x12, waiting for transfers between devices, extended_2(): before = lax.ppermute(last, axis, up)  33.3 us
    all_to_all x1, blocking collectives, shards(): lax.all_to_all(estimate, 'gz', split_axis=2, concat_axis=0, tiled=True)  20.7 us
    ppermute x12, starting transfers between devices, extended_2(): after = lax.ppermute(initial, axis, down)  18.4 us
  transfers between devices with their start and end apart: 24, of which 16 were waited for; matrix products, arithmetic and copies ran while one was open for 16% of the time, Pallas kernels for 0%

commit v1 on v0

v1 whole, which is shorter than its diff:
```python
import functools

import jax
import jax.numpy as jnp
from jax import lax
from jax.experimental import pallas as pl
from jax.experimental.pallas import tpu as pltpu
from jax.sharding import PartitionSpec as P

MESH = pl.DeviceIdType.MESH
F32, BF16 = jnp.float32, jnp.bfloat16
CHUNKS = 4
TILES = 4 // CHUNKS
DEPTH = 32 // CHUNKS


def split(value):
    high = value.astype(BF16)
    return high, (value - high.astype(F32)).astype(BF16)


def dot(a, b):
    return jnp.dot(a, b, preferred_element_type=F32)


def left_product(matrix, value):
    high, low = split(value)
    return dot(matrix[0], high) + (dot(matrix[1], high) + dot(matrix[0], low))


def right_product(value, matrix):
    high, low = split(value)
    return dot(high, matrix[0]) + (dot(high, matrix[1]) + dot(low, matrix[0]))


def toeplitz(taps, count, rows, width, first, step):
    lane = lax.broadcasted_iota(jnp.int32, (8, width), 1)
    base = jnp.zeros((8, width), F32)
    total = taps[0]
    for s in range(count):
        base = jnp.where(lane == first + step * s, taps[s], base)
        if s:
            total = total + taps[s]
    base = base / jnp.full((8, width), total, F32)
    spread = jnp.broadcast_to(base[0:1], (rows, width))
    return pltpu.roll(spread, 0, 1, stride=1, stride_axis=0)


def store_split(ref, value):
    high, low = split(value)
    ref[0] = high
    ref[1] = low


def y_matrix(ref, taps, first, step):
    full = toeplitz(taps, 31, 256, 256, first, step)[:, 0:128]
    high, low = split(full)
    for i, part in enumerate((high, low)):
        ref[i, 0:128] = part[16:144]
        ref[i, 128:144] = part[0:16]
        ref[i, 144:160] = part[144:160]
        ref[i, 160:256] = jnp.zeros((96, 128), BF16)


def pack_edges(value):
    lane = lax.broadcasted_iota(jnp.int32, (32, 128), 1) // 16
    upper, lower = None, None
    for k in range(8):
        rows = value[32 * k:32 * k + 32]
        up = pltpu.roll(rows, (16 * k + 16) % 128, 1)
        down = pltpu.roll(rows, 16 * k, 1) if k else rows
        upper = up if upper is None else jnp.where(lane == k, up, upper)
        lower = down if lower is None else jnp.where(lane == k, down, lower)
    return upper, lower


def unpack_edges(left, right):
    lane = lax.broadcasted_iota(jnp.int32, (32, 128), 1)
    rows = []
    for k in range(8):
        a = pltpu.roll(left, (128 - 16 * k) % 128, 1) if k else left
        b = pltpu.roll(right, (128 - 16 * k + 16) % 128, 1)
        rows.append(jnp.where(lane < 16, a, b))
    return jnp.concatenate(rows, axis=0)


def kernel(obs_ref, px, py, pz, est_ref, two_ref, four_ref, eight_ref,
           xf, xa, yf, ya, zf, za, obsx, obsb, u, v, zb, rb, wb, w, wyx0, wyx1, est2, est3,
           yfs, yfr, yas, yar, pooled_z, pooled_t, sent_two, got_two, part_four,
           sx_s, sx_r, sy_s, sy_r, sa_s, sa_r, so_s, so_r, sp_s, sp_r):
    gx, gy, gz = lax.axis_index("gx"), lax.axis_index("gy"), lax.axis_index("gz")
    x_sides = ((gx > 0, {"gx": gx - 1}), (gx < 3, {"gx": gx + 1}))
    y_sides = ((gy > 0, {"gy": gy - 1}), (gy < 3, {"gy": gy + 1}))

    obsx[0:16] = jnp.zeros((16, 32, 128), F32)
    obsx[48:64] = jnp.zeros((16, 32, 128), F32)
    for t in range(2):
        for j in range(2):
            zb[t, j, 0:64] = jnp.zeros((64, 128), F32)
            zb[t, j, 576:640] = jnp.zeros((64, 128), F32)
        for side in range(2):
            yfr[t, side] = jnp.zeros((128, 128), F32)
            yar[t, side] = jnp.zeros((128, 128), F32)
    for j in range(2):
        rb[j, 0:64] = jnp.zeros((64, 128), F32)
        rb[j, 576:640] = jnp.zeros((64, 128), F32)
    wyx0[0:32] = jnp.zeros((32, 32, 128), F32)
    wyx0[64:96] = jnp.zeros((32, 32, 128), F32)
    wyx1[0:16] = jnp.zeros((16, 32, 128), F32)
    wyx1[48:64] = jnp.zeros((16, 32, 128), F32)

    barrier = pltpu.get_barrier_semaphore()

    def greet(k, carry):
        pl.semaphore_signal(barrier, inc=1, device_id={"gz": lax.rem(gz + k, 16)}, device_id_type=MESH)
        return carry

    lax.fori_loop(1, 16, greet, 0)
    for there, target in x_sides + y_sides:
        @pl.when(there)
        def _():
            pl.semaphore_signal(barrier, inc=1, device_id=target, device_id_type=MESH)

    for x in range(32):
        obsx[16 + x] = obs_ref[pl.ds(x, 32, stride=32), :]
    store_split(xf, toeplitz(px, 31, 256, 512, 8, 8))

    neighbours = sum(there.astype(jnp.int32) for there, _ in x_sides + y_sides)
    pl.semaphore_wait(barrier, 15 + neighbours)

    def x_copy(phase, side, c):
        z = pl.ds(DEPTH * c, DEPTH)
        if phase == 0:
            buffer, own, width, low, high = obsx, 16, 15, 1, 48
        elif phase == 1:
            buffer, own, width, low, high = wyx0, 32, 30, 2, 64
        else:
            buffer, own, width, low, high = wyx1, 16, 15, 1, 48
        source = own if side == 0 else own + 32 - width
        target = high if side == 0 else low
        return pltpu.make_async_remote_copy(
            src_ref=buffer.at[pl.ds(source, width), z], dst_ref=buffer.at[pl.ds(target, width), z],
            send_sem=sx_s.at[phase, side, c], recv_sem=sx_r.at[phase, side, c],
            device_id=x_sides[side][1], device_id_type=MESH)

    def y_copy(phase, side, c):
        t = phase // 2
        sent, got = (yfs, yfr) if phase % 2 == 0 else (yas, yar)
        rows = pl.ds(32 * TILES * c, 32 * TILES)
        return pltpu.make_async_remote_copy(
            src_ref=sent.at[t, side, rows], dst_ref=got.at[t, 1 - side, rows],
            send_sem=sy_s.at[phase, side, c], recv_sem=sy_r.at[phase, 1 - side, c],
            device_id=y_sides[side][1], device_id_type=MESH)

    def start(sides, copy, phase, c):
        for side in range(2):
            @pl.when(sides[side][0])
            def _():
                copy(phase, side, c).start()

    def arrive(sides, copy, phase, c):
        for side in range(2):
            @pl.when(sides[side][0])
            def _():
                copy(phase, 1 - side, c).wait_recv()

    def depart(sides, copy, phase, c):
        for side in range(2):
            @pl.when(sides[side][0])
            def _():
                copy(phase, side, c).wait_send()

    def everyone(source, target, send_sem, recv_sem):
        def one(k, carry):
            d = lax.rem(gz + k, 16)
            pltpu.make_async_remote_copy(
                src_ref=source(d), dst_ref=target, send_sem=send_sem, recv_sem=recv_sem,
                device_id={"gz": d}, device_id_type=MESH).start()
            return carry
        lax.fori_loop(1, 16, one, 0)

    def await_bytes(ref, sem):
        pltpu.make_async_copy(ref, ref, sem).wait()

    def columns(ref, first, count, c):
        parts = [ref[first:first + count, DEPTH * c + 8 * j:DEPTH * c + 8 * j + 8, :].reshape(8 * count, 128)
                 for j in range(TILES)]
        return parts[0] if TILES == 1 else jnp.concatenate(parts, axis=1)

    def tile(value, j):
        return value[:, 128 * j:128 * j + 128]

    def pack_and_send(value, phase, c):
        t = phase // 2
        sent = yfs if phase % 2 == 0 else yas
        for j in range(TILES):
            upper, lower = pack_edges(tile(value, j))
            rows = slice(32 * (TILES * c + j), 32 * (TILES * c + j) + 32)
            sent[t, 0, rows] = lower
            sent[t, 1, rows] = upper
        start(y_sides, y_copy, phase, c)

    def blur_y(source, phase, c, matrix, target, first):
        t = phase // 2
        got = yfr if phase % 2 == 0 else yar
        arrive(y_sides, y_copy, phase, c)
        for j in range(TILES):
            z = slice(DEPTH * c + 8 * j, DEPTH * c + 8 * j + 8)
            rows = slice(32 * (TILES * c + j), 32 * (TILES * c + j) + 32)
            halo = unpack_edges(got[t, 0, rows], got[t, 1, rows])
            own = source[:, z, :].reshape(256, 128)
            result = right_product(jnp.concatenate([own, halo], axis=1), matrix)
            target[first:first + 32, z, :] = result.reshape(32, 8, 128)

    def forward_end(t, c):
        blur_y(u, 2 * t, c, yf, v.at[t], 0)
        z = pl.ds(DEPTH * c, DEPTH)
        place = pl.ds(pl.multiple_of(64 + 32 * gz + DEPTH * c, 8), DEPTH)
        everyone(lambda d: v.at[t, pl.ds(2 * d, 2), z], zb.at[t, :, place], sa_s.at[t, 0], sa_r.at[t, 0])
        zb[t, :, place, :] = v[t, pl.ds(2 * gz, 2), z, :]

    def blur_x(matrix, ref, first, c):
        return left_product(matrix, columns(ref, first, 64, c))

    def store_columns(ref, first, value, c):
        for j in range(TILES):
            z = slice(DEPTH * c + 8 * j, DEPTH * c + 8 * j + 8)
            ref[first:first + 32, z, :] = tile(value, j).reshape(32, 8, 128)

    def middle(t):
        await_bytes(zb.at[t, :, pl.ds(0, 480)], sa_r.at[t, 0])
        for b in range(4):
            window = jnp.concatenate([zb[t, j, 128 * b:128 * b + 256, :] for j in range(2)], axis=1)
            blurred = left_product(zf, window)
            for j in range(2):
                rb[j, 64 + 128 * b:192 + 128 * b] = obsb[j, 128 * b:128 * b + 128, :] / tile(blurred, j)
        for b in range(4):
            window = jnp.concatenate([rb[j, 128 * b:128 * b + 256, :] for j in range(2)], axis=1)
            back = left_product(za, window)
            for j in range(2):
                wb[t, j, 128 * b:128 * b + 128] = tile(back, j)
        mine = pl.ds(2 * gz, 2)
        for c in range(CHUNKS):
            everyone(lambda d: wb.at[t, :, pl.ds(pl.multiple_of(32 * d + DEPTH * c, 8), DEPTH)],
                     w.at[t, mine, pl.ds(DEPTH * c, DEPTH)], sa_s.at[t, 1], sa_r.at[t, 1 + c])
        w[t, mine] = wb[t, :, pl.ds(pl.multiple_of(32 * gz, 8), 32), :]

    def back_y(t, c):
        await_bytes(w.at[t, pl.ds(0, 30), pl.ds(0, DEPTH)], sa_r.at[t, 1 + c])
        pack_and_send(columns(w.at[t], 0, 32, c), 2 * t + 1, c)

    for c in range(CHUNKS):
        start(x_sides, x_copy, 0, c)
    everyone(lambda d: obsx.at[pl.ds(16 + 2 * d, 2)], obsb.at[:, pl.ds(pl.multiple_of(32 * gz, 8), 32)],
             so_s, so_r)
    obsb[:, pl.ds(pl.multiple_of(32 * gz, 8), 32), :] = obsx[pl.ds(16 + 2 * gz, 2)]
    y_matrix(yf, py, 255, -1)
    store_split(zf, toeplitz(pz, 61, 128, 256, 34, 1))
    store_split(za, toeplitz(pz, 61, 128, 256, 94, -1))
    store_split(xa, toeplitz(px, 31, 256, 512, 248, -8))
    y_matrix(ya, py, 225, 1)

    for i in range(CHUNKS + 1):
        if i < CHUNKS:
            arrive(x_sides, x_copy, 0, i)
            value = blur_x(xf, obsx, 0, i)
            store_columns(u, 0, value, i)
            pack_and_send(value, 0, i)
        if i >= 1:
            forward_end(0, i - 1)
    await_bytes(obsb.at[:, pl.ds(0, 480)], so_r)
    middle(0)

    for i in range(CHUNKS + 3):
        if i < CHUNKS:
            back_y(0, i)
        if 0 <= i - 1 < CHUNKS:
            blur_y(w.at[0], 1, i - 1, ya, wyx0, 32)
            start(x_sides, x_copy, 1, i - 1)
        if 0 <= i - 2 < CHUNKS:
            c = i - 2
            arrive(x_sides, x_copy, 1, c)
            for half in range(2):
                correction = blur_x(xa, wyx0, 32 * half, c)
                store_columns(est2, 32 * half, columns(obsx, 32 * half, 32, c) * correction, c)
            value = blur_x(xf, est2, 0, c)
            depart(y_sides, y_copy, 0, c)
            store_columns(u, 0, value, c)
            pack_and_send(value, 2, c)
        if i >= 3:
            forward_end(1, i - 3)
    middle(1)

    for i in range(CHUNKS + 2):
        if i < CHUNKS:
            back_y(1, i)
        if 0 <= i - 1 < CHUNKS:
            blur_y(w.at[1], 3, i - 1, ya, wyx1, 16)
            start(x_sides, x_copy, 2, i - 1)
        if i >= 2:
            c = i - 2
            arrive(x_sides, x_copy, 2, c)
            correction = blur_x(xa, wyx1, 0, c)
            for j in range(TILES):
                z = slice(DEPTH * c + 8 * j, DEPTH * c + 8 * j + 8)
                new = est2[16:48, z, :] * tile(correction, j).reshape(32, 8, 128)
                for x in range(32):
                    est3[32 * x + z.start:32 * x + z.stop] = new[x]
                for x in range(16):
                    pooled_z[32 * x + z.start:32 * x + z.stop] = new[2 * x] + new[2 * x + 1]

    halves = pooled_z[pl.ds(0, 256, stride=2), :] + pooled_z[pl.ds(1, 256, stride=2), :]
    for half in range(2):
        pooled_t[half] = jnp.transpose(halves[128 * half:128 * half + 128])
        even, odd = pooled_t[half, pl.ds(0, 64, stride=2), :], pooled_t[half, pl.ds(1, 64, stride=2), :]
        level = (even + odd) * 0.125
        for d in range(16):
            sent_two[d, 4 * half:4 * half + 4] = level[4 * d:4 * d + 4]
    everyone(lambda d: sent_two.at[d], got_two.at[gz], sp_s, sp_r)
    got_two[gz] = sent_two[gz]
    for z in range(32):
        est_ref[32 * z:32 * z + 32] = est3[pl.ds(z, 32, stride=32), :]
    await_bytes(got_two.at[pl.ds(0, 15)], sp_r)
    group = lax.broadcasted_iota(jnp.int32, (8, 128), 1) // 16
    for half in range(2):
        blocks = [got_two[8 * half + s] for s in range(8)]
        for bit in range(3):
            step = 1 << bit
            upper = (group & step) != 0
            for s in range(8):
                if s & step == 0:
                    a, b = blocks[s], blocks[s + step]
                    blocks[s] = jnp.where(upper, pltpu.roll(b, 16 * step, 1), a)
                    blocks[s + step] = jnp.where(upper, b, pltpu.roll(a, 128 - 16 * step, 1))
        for x in range(8):
            two_ref[x, :, 128 * half:128 * half + 128] = blocks[x][0:4]
            two_ref[8 + x, :, 128 * half:128 * half + 128] = blocks[x][4:8]

    def pool_matrix(rows):
        r = lax.broadcasted_iota(jnp.int32, (rows, rows // 2), 0)
        c = lax.broadcasted_iota(jnp.int32, (rows, rows // 2), 1)
        return jnp.where(r // 2 == c, 0.125, 0.0).astype(F32)

    for a in range(8):
        s = two_ref[2 * a] + two_ref[2 * a + 1]
        part_four[2 * a:2 * a + 1] = s[0:1] + s[1:2]
        part_four[2 * a + 1:2 * a + 2] = s[2:3] + s[3:4]
    four = jnp.dot(part_four[...], pool_matrix(256), precision=lax.Precision.HIGHEST, preferred_element_type=F32)
    for a in range(8):
        four_ref[a] = four[2 * a:2 * a + 2]
    rows = [four[4 * a:4 * a + 1] + four[4 * a + 1:4 * a + 2] + four[4 * a + 2:4 * a + 3] + four[4 * a + 3:4 * a + 4]
            for a in range(4)]
    eight = jnp.dot(jnp.concatenate(rows + rows, axis=0), pool_matrix(128),
                    precision=lax.Precision.HIGHEST, preferred_element_type=F32)
    for a in range(4):
        eight_ref[a] = eight[a:a + 1]

    for c in range(CHUNKS):
        for phase in range(3):
            depart(x_sides, x_copy, phase, c)
        for phase in range(1, 4):
            depart(y_sides, y_copy, phase, c)
    for t in range(2):
        await_bytes(zb.at[t, :, pl.ds(0, 480)], sa_s.at[t, 0])
        await_bytes(wb.at[t, :, pl.ds(0, 480)], sa_s.at[t, 1])
    await_bytes(obsb.at[:, pl.ds(0, 480)], so_s)
    await_bytes(sent_two.at[pl.ds(0, 15)], sp_s)


def shards(observed, profile_x, profile_y, profile_z):
    vmem = pl.BlockSpec(memory_space=pltpu.VMEM)
    smem = pl.BlockSpec(memory_space=pltpu.SMEM)
    dma = pltpu.SemaphoreType.DMA
    estimate, two, four, eight = pl.pallas_call(
        kernel,
        out_shape=[
            jax.ShapeDtypeStruct((1024, 128), F32),
            jax.ShapeDtypeStruct((16, 4, 256), F32),
            jax.ShapeDtypeStruct((8, 2, 128), F32),
            jax.ShapeDtypeStruct((4, 1, 64), F32),
        ],
        in_specs=[vmem, smem, smem, smem],
        out_specs=[vmem] * 4,
        scratch_shapes=[
            pltpu.VMEM((2, 256, 512), BF16),
            pltpu.VMEM((2, 256, 512), BF16),
            pltpu.VMEM((2, 256, 128), BF16),
            pltpu.VMEM((2, 256, 128), BF16),
            pltpu.VMEM((2, 128, 256), BF16),
            pltpu.VMEM((2, 128, 256), BF16),
            pltpu.VMEM((64, 32, 128), F32),
            pltpu.VMEM((2, 512, 128), F32),
            pltpu.VMEM((32, 32, 128), F32),
            pltpu.VMEM((2, 32, 32, 128), F32),
            pltpu.VMEM((2, 2, 640, 128), F32),
            pltpu.VMEM((2, 640, 128), F32),
            pltpu.VMEM((2, 2, 512, 128), F32),
            pltpu.VMEM((2, 32, 32, 128), F32),
            pltpu.VMEM((96, 32, 128), F32),
            pltpu.VMEM((64, 32, 128), F32),
            pltpu.VMEM((64, 32, 128), F32),
            pltpu.VMEM((1024, 128), F32),
            pltpu.VMEM((2, 2, 128, 128), F32),
            pltpu.VMEM((2, 2, 128, 128), F32),
            pltpu.VMEM((2, 2, 128, 128), F32),
            pltpu.VMEM((2, 2, 128, 128), F32),
            pltpu.VMEM((512, 128), F32),
            pltpu.VMEM((2, 128, 128), F32),
            pltpu.VMEM((16, 8, 128), F32),
            pltpu.VMEM((16, 8, 128), F32),
            pltpu.VMEM((16, 256), F32),
            dma((3, 2, CHUNKS)), dma((3, 2, CHUNKS)),
            dma((4, 2, CHUNKS)), dma((4, 2, CHUNKS)),
            dma((2, 2)), dma((2, 1 + CHUNKS)),
            dma, dma, dma, dma,
        ],
        compiler_params=pltpu.CompilerParams(
            collective_id=0, has_side_effects=True, vmem_limit_bytes=48 * 1024 * 1024),
        name="deconvolve",
    )(observed.reshape(1024, 128), profile_x, profile_y, profile_z)
    return estimate.reshape(32, 32, 128), two, four, eight


def solution(mesh):
    return jax.shard_map(
        shards,
        mesh=mesh,
        in_specs=(P("gz", "gx", "gy"), P(), P(), P()),
        out_specs=(
            P("gz", "gx", "gy"),
            P("gx", ("gy", "gz"), None),
            P("gx", ("gy", "gz"), None),
            P("gx", ("gy", "gz"), None),
        ),
        check_vma=False,
    )
```

time: 414 us -> 102 us (0.25)
  local copies, waits for them, and re-layouts: 113 us -> 4.3 us
  Pallas kernels: 0 us -> 97.1 us
  matrix products: 93.3 us -> 0 us
  waiting for transfers between devices: 80.1 us -> 0 us
  starting transfers between devices: 77.6 us -> 0 us
  other arithmetic: 25.7 us -> 0 us
  blocking collectives: 20.7 us -> 0 us
    pallas_call x0 -> x1, Pallas kernels: none -> 97.1 us  [shards(): pl.pallas_call(kernel, out_shape=[jax.ShapeDtypeStruct((1024, 128), F32),...]
    dot_general x12 -> x0, matrix products: 93.3 us -> none  [the longest x4 84.2 us: along_y(): jnp.einsum('zxr,rc->zxc', extended, matrix, precision=lax.Precision.HIGHEST)]
    ppermute x24 -> x0, waiting for transfers between devices: 80.1 us -> none  [the longest x12 46.8 us: extended_2(): after = lax.ppermute(initial, axis, down)]
    ppermute x24 -> x0, starting transfers between devices: 77.6 us -> none  [the longest x12 59.1 us: extended_2(): before = lax.ppermute(last, axis, up)]
    gather x10 -> x0, local copies, waits for them, and re-layouts: 60 us -> none  [band_matrix(): picked = kernel[jnp.clip(which, 0, tap_count - 1)]]
    reshape x1 -> x0, local copies, waits for them, and re-layouts: 34.8 us -> none  [pool_half(): field.reshape(sx // 2, 2, sy // 2, 2, sz // 2, 2).mean(axis=(1, 3, 5))]
    all_to_all x1 -> x0, blocking collectives: 20.7 us -> none  [shards(): lax.all_to_all(estimate, 'gz', split_axis=2, concat_axis=0, tiled=True)]
    reduce_sum x7 -> x0, other arithmetic: 18.6 us -> none  [the longest x4 14.9 us: pool_half(): field.reshape(sx // 2, 2, sy // 2, 2, sz // 2, 2).mean(axis=(1, 3, 5))]
  transfers between devices with their start and end apart: 24 -> 0, of which waited for: 16 -> 0; matrix products, arithmetic and copies ran while one was open for 16% -> 0% of each run, Pallas kernels for 0% -> 0%
where the time goes in v1:
time: 102 us
  Pallas kernels  97.1 us (95%)
  local copies, waits for them, and re-layouts  4.3 us (4%)
    pallas_call x1, Pallas kernels, shards(): pl.pallas_call(kernel, out_shape=[jax.ShapeDtypeStruct((1024, 128), F32),...  97.1 us
    unnamed x12, local copies, waits for them, and re-layouts  4.3 us

profile of v1, /device:TPU:1, one launch (start us, length us, event | category | flops | bytes accessed | tf_op | source)
XLA Modules:
  0.0 102.0 jit_solution(5300524863052870964)
XLA Ops:
  0.6 0.0 copy-start.3
  0.6 0.0 copy-start.2
  0.7 0.0 copy-start.1
  0.7 0.6 copy-done.3
  1.3 0.0 copy-done.2
  1.3 0.0 copy-done.1
  1.3 0.0 copy-start
  1.3 1.0 %copy-done = f32[32,32,128]{2,1,0:T(8,128)S(1)} copy-done((f32[32,32,128]{2,1,0:T(8,128)S(1)}, f32[32,32,128]{2,1,0:T(8,128)}, u32[]{:S(2)}) %copy-start) | copy-done | bytes 524312
  2.4 97.1 %deconvolve.1 = (f32[1024,128]{1,0:T(8,128)S(1)}, f32[16,4,256]{2,1,0:T(4,128)S(1)}, f32[8,2,128]{2,1,0:T(2,128)S(1)}, f32[4,1,64]{2,1,0:T(1,128)S(1)}) custom-call(f32[1024,128]{1,0:T(8,128)S(1)} %bitcast.2, f32[31]{0:T(128)S(1)} %copy-done.1, f32[31]{0:T(128)S(1)} %copy-done.2, f32[61]{0:T(128)S(1)} %copy-done.3), custom_call_target="tpu_custom_call" | custom-call | tf_op jit(solution)/shard_map/deconvolve/pallas_call | solution.py:374
  99.4 0.8 copy.12
  100.2 0.6 copy.13
  100.9 0.6 copy.14
  101.5 0.6 copy.15
Async XLA Ops:
  0.6 0.7 copy-start.3
  0.6 0.7 copy-start.2
  0.7 0.7 copy-start.1
  1.3 1.0 %copy-start = (f32[32,32,128]{2,1,0:T(8,128)S(1)}, f32[32,32,128]{2,1,0:T(8,128)}, u32[]{:S(2)}) copy-start(f32[32,32,128]{2,1,0:T(8,128)} %param.4) | copy-start | bytes 1572868

commit v2 on v0

v2 whole, which is shorter than its diff:
```python
import functools

import jax
import jax.numpy as jnp
from jax import lax
from jax.experimental import pallas as pl
from jax.experimental.pallas import tpu as pltpu
from jax.sharding import PartitionSpec as P

MESH = pl.DeviceIdType.MESH
F32, BF16 = jnp.float32, jnp.bfloat16
CHUNKS = 2
TILES = 4 // CHUNKS
DEPTH = 32 // CHUNKS


def split(value):
    high = value.astype(BF16)
    return high, (value - high.astype(F32)).astype(BF16)


def dot(a, b):
    return jnp.dot(a, b, preferred_element_type=F32)


def left_product(matrix, value):
    high, low = split(value)
    return dot(matrix[0], high) + (dot(matrix[1], high) + dot(matrix[0], low))


def right_product(value, matrix):
    high, low = split(value)
    return dot(high, matrix[0]) + (dot(high, matrix[1]) + dot(low, matrix[0]))


def toeplitz(taps, count, rows, width, first, step):
    lane = lax.broadcasted_iota(jnp.int32, (8, width), 1)
    base = jnp.zeros((8, width), F32)
    total = taps[0]
    for s in range(count):
        base = jnp.where(lane == first + step * s, taps[s], base)
        if s:
            total = total + taps[s]
    base = base / jnp.full((8, width), total, F32)
    spread = jnp.broadcast_to(base[0:1], (rows, width))
    return pltpu.roll(spread, 0, 1, stride=1, stride_axis=0)


def store_split(ref, value):
    high, low = split(value)
    ref[0] = high
    ref[1] = low


def y_forward(ref, taps):
    full = toeplitz(taps, 31, 256, 256, 255, -1)
    lane = lax.broadcasted_iota(jnp.int32, (256, 128), 1) // 16
    own = pltpu.roll(full, 240, 1)[:, 0:128]
    for j in range(2):
        left = pltpu.roll(full, 16 * j, 1)[:, 0:128] if j else full[:, 0:128]
        right = pltpu.roll(full, 144 + 16 * j, 1)[:, 0:128]
        side = jnp.where(lane == j, left, jnp.where(lane == 2 + j, right, 0.0))
        for i, part in enumerate(split(jnp.concatenate([own, side], axis=1))):
            ref[j, i, 0:128] = part[32:160]
            ref[j, i, 128:160] = part[0:32]
            ref[j, i, 160:192] = part[160:192]
            ref[j, i, 192:256] = jnp.zeros((64, 256), BF16)


def y_adjoint(ref, taps):
    full = toeplitz(taps, 31, 256, 256, 225, 1)[:, 0:128]
    for i, part in enumerate(split(full)):
        for j in range(2):
            ref[j, i, 128:256] = jnp.zeros((128, 128), BF16)
            ref[j, i, 0:128] = part[16:144]
            ref[j, i, 128 + 16 * j:144 + 16 * j] = part[0:16]
            ref[j, i, 160 + 16 * j:176 + 16 * j] = part[144:160]


def gather_lanes(parts, width, first):
    lane = lax.broadcasted_iota(jnp.int32, parts[0].shape, 1) // width
    result = None
    for k, part in enumerate(parts):
        shift = (width * k - first) % 128
        moved = pltpu.roll(part, shift, 1) if shift else part
        result = moved if result is None else jnp.where(lane == k, moved, result)
    return result


def spread_lanes(left, right, width, k):
    lane = lax.broadcasted_iota(jnp.int32, left.shape, 1)
    a, b = (128 - width * k) % 128, (width - width * k) % 128
    left = pltpu.roll(left, a, 1) if a else left
    right = pltpu.roll(right, b, 1) if b else right
    return jnp.where(lane < width, left, right)


def kernel(obs_ref, px, py, pz, est_ref, two_ref, four_ref, eight_ref,
           xf, xa, yf, ya, zf, za, obsx, obsb, obss, obse_s, obse_r, u, um, ue_s, ue_r, zb, rb, wb,
           wyx0, wyx1, est2, est3, pooled_z, pooled_t, sent_two, got_two, part_four,
           sx_s, sx_r, sn_s, sn_r, sf_s, sf_r, se_s, se_r, sa_s, sa_r, so_s, so_r, sp_s, sp_r):
    gx, gy, gz = lax.axis_index("gx"), lax.axis_index("gy"), lax.axis_index("gz")
    x_sides = ((gx > 0, {"gx": gx - 1}), (gx < 3, {"gx": gx + 1}))
    y_sides = ((gy > 0, gy - 1), (gy < 3, gy + 1))
    inner = (gx == 1) | (gx == 2)
    parity = lax.rem(gx, 2)

    obsx[0, 0] = jnp.zeros((32, 128), F32)
    obsx[3, 15] = jnp.zeros((32, 128), F32)

    @pl.when(gx == 0)
    def _():
        obsx[0] = jnp.zeros((16, 32, 128), F32)
        wyx0[0:2] = jnp.zeros((2, 16, 32, 128), F32)
        wyx1[0] = jnp.zeros((16, 32, 128), F32)

    @pl.when(gx == 3)
    def _():
        obsx[3] = jnp.zeros((16, 32, 128), F32)
        wyx0[4:6] = jnp.zeros((2, 16, 32, 128), F32)
        wyx1[3] = jnp.zeros((16, 32, 128), F32)

    for side in range(2):
        @pl.when(jnp.logical_not(y_sides[side][0]))
        def _():
            obse_r[side] = jnp.zeros((16, 8, 128), F32)
            for t in range(2):
                ue_r[t, side] = jnp.zeros((CHUNKS, 16, 8, 128), F32)

    barrier = pltpu.get_barrier_semaphore()

    def greet(target):
        pl.semaphore_signal(barrier, inc=1, device_id=target, device_id_type=MESH)

    def others(body):
        def one(k, carry):
            body(lax.rem(gz + k, 16))
            return carry
        lax.fori_loop(1, 16, one, 0)

    def everyone(body):
        def one(k, carry):
            body(lax.rem(gz + k, 16))
            return carry
        lax.fori_loop(0, 16, one, 0)

    greet({"gx": gx + 1 - 2 * parity})

    @pl.when(inner)
    def _():
        everyone(lambda d: greet({"gx": 3 - gx, "gz": d}))
    others(lambda d: greet({"gz": d}))
    for there, target in y_sides:
        @pl.when(there)
        def _():
            everyone(lambda d: greet({"gy": target, "gz": d}))

    for x in range(32):
        obsx[1 + x // 16, x % 16] = obs_ref[pl.ds(x, 32, stride=32), :]

    neighbours = sum(there.astype(jnp.int32) for there, _ in y_sides) + inner.astype(jnp.int32)
    pl.semaphore_wait(barrier, 16 + 16 * neighbours)

    def await_bytes(ref, sem):
        pltpu.make_async_copy(ref, ref, sem).wait()

    def z_of(c):
        return pl.ds(DEPTH * c, DEPTH)

    def x_copy(side, c):
        source = obsx.at[1, pl.ds(0, 15), z_of(c)] if side == 0 else obsx.at[2, pl.ds(1, 15), z_of(c)]
        target = obsx.at[3, pl.ds(0, 15), z_of(c)] if side == 0 else obsx.at[0, pl.ds(1, 15), z_of(c)]
        return pltpu.make_async_remote_copy(
            src_ref=source, dst_ref=target, send_sem=sx_s.at[side, c], recv_sem=sx_r.at[side, c],
            device_id=x_sides[side][1], device_id_type=MESH)

    for c in range(CHUNKS):
        for side in range(2):
            @pl.when(x_sides[side][0])
            def _():
                x_copy(side, c).start()

    def send(source, target, send_sem, recv_sem, device):
        pltpu.make_async_remote_copy(
            src_ref=source, dst_ref=target, send_sem=send_sem, recv_sem=recv_sem,
            device_id=device, device_id_type=MESH).start()

    others(lambda d: send(obsx.at[pl.ds(1, 2), d], obsb.at[:, gz], so_s, so_r, {"gz": d}))
    obsb[:, gz] = obsx[1:3, gz]
    for side, first in ((0, 0), (1, 112)):
        parts = [obsx[1 + j, :, 8 * k:8 * k + 8, :].reshape(128, 128) for k in range(4) for j in range(2)]
        obse_s[side] = gather_lanes(parts, 16, first).reshape(16, 8, 128)

        @pl.when(y_sides[side][0])
        def _():
            everyone(lambda d: send(obse_s.at[side, d], obse_r.at[1 - side, gz], se_s.at[2, side, 0],
                                    se_r.at[2, 1 - side, 0], {"gy": y_sides[side][1], "gz": d}))

    store_split(xf, toeplitz(px, 31, 256, 512, 8, 8))
    y_forward(yf, py)
    store_split(zf, toeplitz(pz, 61, 128, 256, 34, 1))
    store_split(za, toeplitz(pz, 61, 128, 256, 94, -1))
    store_split(xa, toeplitz(px, 31, 256, 512, 248, -8))
    y_adjoint(ya, py)
    for part in range(3):
        for ref in (zb, rb):
            ref[part, 0:2] = jnp.zeros((2, 32, 128), F32)
            ref[part, 18:20] = jnp.zeros((2, 32, 128), F32)

    def columns(ref, first, count, c):
        parts = [ref[first:first + count, :, DEPTH * c + 8 * j:DEPTH * c + 8 * j + 8, :].reshape(128 * count, 128)
                 for j in range(TILES)]
        return parts[0] if TILES == 1 else jnp.concatenate(parts, axis=1)

    def tile(value, j):
        return value[:, 128 * j:128 * j + 128]

    def blur_x(matrix, ref, first, c):
        return left_product(matrix, columns(ref, first, 4, c))

    def store_columns(ref, first, value, c):
        for j in range(TILES):
            z = slice(DEPTH * c + 8 * j, DEPTH * c + 8 * j + 8)
            ref[first:first + 2, :, z, :] = tile(value, j).reshape(2, 16, 8, 128)

    def to_columns(t, value, c):
        store_columns(u.at[t], 0, value, c)
        others(lambda d: send(u.at[t, :, d, z_of(c)], um.at[t, :, gz, z_of(c)], sa_s.at[t, 0], sa_r.at[t, 0, c],
                              {"gz": d}))
        parts = [tile(value, k)[128 * j:128 * j + 128] for k in range(TILES) for j in range(2)]
        for side, first in ((0, 0), (1, 96)):
            ue_s[t, side, c] = gather_lanes(parts, 32, first).reshape(16, 8, 128)

            @pl.when(y_sides[side][0])
            def _():
                everyone(lambda d: send(ue_s.at[t, side, c, d], ue_r.at[t, 1 - side, c, gz], se_s.at[t, side, c],
                                        se_r.at[t, 1 - side, c], {"gy": y_sides[side][1], "gz": d}))
        um[t, :, gz, z_of(c), :] = u[t, :, gz, z_of(c), :]

    def middle(t, own):
        for c in range(CHUNKS):
            await_bytes(um.at[t, :, pl.ds(0, 15), pl.ds(0, DEPTH)], sa_r.at[t, 0, c])
            for side in range(2):
                @pl.when(y_sides[side][0])
                def _():
                    await_bytes(ue_r.at[t, side, c], se_r.at[t, side, c])
            left, right = (ue_r[t, side, c].reshape(128, 128) for side in range(2))
            sides = None
            for j in range(2):
                halo = jnp.concatenate(
                    [spread_lanes(left, right, 32, 2 * k + j).reshape(16, 8, 128) for k in range(TILES)], axis=1)
                own_lanes = um[t, j, :, DEPTH * c:DEPTH * c + DEPTH, :].reshape(16 * DEPTH, 128)
                result = right_product(jnp.concatenate([own_lanes, halo.reshape(16 * DEPTH, 128)], axis=1), yf.at[j])
                zb[j, 2:18, DEPTH * c:DEPTH * c + DEPTH, :] = tile(result, 0).reshape(16, DEPTH, 128)
                sides = tile(result, 1) if sides is None else sides + tile(result, 1)
            zb[2, 2:18, DEPTH * c:DEPTH * c + DEPTH, :] = sides.reshape(16, DEPTH, 128)
        if t == 0:
            await_bytes(obsb.at[:, pl.ds(0, 15)], so_r)
            for side in range(2):
                @pl.when(y_sides[side][0])
                def _():
                    await_bytes(obse_r.at[side], se_r.at[2, side, 0])
            left, right = (obse_r[side].reshape(128, 128) for side in range(2))
            lane = lax.broadcasted_iota(jnp.int32, (128, 128), 1)
            for k in range(4):
                part = spread_lanes(left, right, 32, k)
                obss[:, 8 * k:8 * k + 8, :] = jnp.where(lane < 64, part, 0.0).reshape(16, 8, 128)
        lane = lax.broadcasted_iota(jnp.int32, (128, 128), 1)
        inside = ((lane < 32) & (gy > 0)) | ((lane >= 32) & (lane < 64) & (gy < 3))
        for b in range(4):
            window = jnp.concatenate([zb[j, 4 * b:4 * b + 8].reshape(256, 128) for j in range(3)], axis=1)
            blurred = left_product(zf, window)
            for j in range(2):
                ratio = obsb[j, 4 * b:4 * b + 4].reshape(128, 128) / tile(blurred, j)
                rb[j, 2 + 4 * b:6 + 4 * b] = ratio.reshape(4, 32, 128)
            ratio = obss[4 * b:4 * b + 4].reshape(128, 128) / jnp.where(inside, tile(blurred, 2), 1.0)
            rb[2, 2 + 4 * b:6 + 4 * b] = jnp.where(inside, ratio, 0.0).reshape(4, 32, 128)
        for b in range(4):
            window = jnp.concatenate([rb[j, 4 * b:4 * b + 8].reshape(256, 128) for j in range(3)], axis=1)
            back = left_product(za, window)
            for j in range(2):
                result = right_product(jnp.concatenate([tile(back, j), tile(back, 2)], axis=1), ya.at[j])
                wb[t, j, 4 * b:4 * b + 4] = result.reshape(4, 32, 128)
        for c in range(CHUNKS):
            @pl.when(inner)
            def _():
                if t == 0:
                    first = 4 * (gx - 1)
                    everyone(lambda d: send(wb.at[t, :, d, z_of(c)], own.at[pl.ds(first, 2), gz, z_of(c)],
                                            sf_s.at[t], sf_r.at[t, c], {"gx": 3 - gx, "gz": d}))
                else:
                    first = 3 * (gx - 1)
                    everyone(lambda d: send(wb.at[t, 2 - gx, d, z_of(c)], own.at[first, gz, z_of(c)],
                                            sf_s.at[t], sf_r.at[t, c], {"gx": 3 - gx, "gz": d}))
            others(lambda d: send(wb.at[t, :, d, z_of(c)], own.at[pl.ds(2 - t, 2), gz, z_of(c)],
                                  sa_s.at[t, 1], sa_r.at[t, 1, c], {"gz": d}))
        own[2 - t:4 - t, gz] = wb[t, :, gz]

    def near_copy(t, ref, c):
        if t == 0:
            source, target = ref.at[pl.ds(2, 2), :, z_of(c)], ref.at[pl.ds(4 * parity, 2), :, z_of(c)]
        else:
            source, target = ref.at[2 - parity, :, z_of(c)], ref.at[3 * parity, :, z_of(c)]
        return pltpu.make_async_remote_copy(
            src_ref=source, dst_ref=target, send_sem=sn_s.at[t, c], recv_sem=sn_r.at[t, c],
            device_id={"gx": gx + 1 - 2 * parity}, device_id_type=MESH)

    def arrive_own(t, ref, c):
        await_bytes(ref.at[pl.ds(2 - t, 2), pl.ds(0, 15), pl.ds(0, DEPTH)], sa_r.at[t, 1, c])
        near_copy(t, ref, c).start()

    def arrive_halos(t, ref, c):
        near_copy(t, ref, c).wait_recv()

        @pl.when(inner)
        def _():
            await_bytes(ref.at[pl.ds(0, 2 - t), :, pl.ds(0, DEPTH)], sf_r.at[t, c])

    for c in range(CHUNKS):
        for side in range(2):
            @pl.when(x_sides[side][0])
            def _():
                x_copy(1 - side, c).wait_recv()
        to_columns(0, blur_x(xf, obsx, 0, c), c)
    middle(0, wyx0)

    for c in range(CHUNKS):
        arrive_own(0, wyx0, c)
    for c in range(CHUNKS):
        arrive_halos(0, wyx0, c)
        for half in range(2):
            correction = blur_x(xa, wyx0, 2 * half, c)
            store_columns(est2, 2 * half, columns(obsx, 2 * half, 2, c) * correction, c)
        to_columns(1, blur_x(xf, est2, 0, c), c)
    middle(1, wyx1)

    for c in range(CHUNKS):
        arrive_own(1, wyx1, c)
    for c in range(CHUNKS):
        arrive_halos(1, wyx1, c)
        correction = blur_x(xa, wyx1, 0, c)
        for j in range(TILES):
            z = slice(DEPTH * c + 8 * j, DEPTH * c + 8 * j + 8)
            new = est2[1:3, :, z, :].reshape(32, 8, 128) * tile(correction, j).reshape(32, 8, 128)
            for x in range(32):
                est3[32 * x + z.start:32 * x + z.stop] = new[x]
            for x in range(16):
                pooled_z[32 * x + z.start:32 * x + z.stop] = new[2 * x] + new[2 * x + 1]

    halves = pooled_z[pl.ds(0, 256, stride=2), :] + pooled_z[pl.ds(1, 256, stride=2), :]
    for half in range(2):
        pooled_t[half] = jnp.transpose(halves[128 * half:128 * half + 128])
        even, odd = pooled_t[half, pl.ds(0, 64, stride=2), :], pooled_t[half, pl.ds(1, 64, stride=2), :]
        level = (even + odd) * 0.125
        for d in range(16):
            sent_two[d, 4 * half:4 * half + 4] = level[4 * d:4 * d + 4]
    others(lambda d: send(sent_two.at[d], got_two.at[gz], sp_s, sp_r, {"gz": d}))
    got_two[gz] = sent_two[gz]
    for z in range(32):
        est_ref[32 * z:32 * z + 32] = est3[pl.ds(z, 32, stride=32), :]
    await_bytes(got_two.at[pl.ds(0, 15)], sp_r)
    group = lax.broadcasted_iota(jnp.int32, (8, 128), 1) // 16
    for half in range(2):
        blocks = [got_two[8 * half + s] for s in range(8)]
        for bit in range(3):
            step = 1 << bit
            upper = (group & step) != 0
            for s in range(8):
                if s & step == 0:
                    a, b = blocks[s], blocks[s + step]
                    blocks[s] = jnp.where(upper, pltpu.roll(b, 16 * step, 1), a)
                    blocks[s + step] = jnp.where(upper, b, pltpu.roll(a, 128 - 16 * step, 1))
        for x in range(8):
            two_ref[x, :, 128 * half:128 * half + 128] = blocks[x][0:4]
            two_ref[8 + x, :, 128 * half:128 * half + 128] = blocks[x][4:8]

    def pool_matrix(rows):
        r = lax.broadcasted_iota(jnp.int32, (rows, rows // 2), 0)
        c = lax.broadcasted_iota(jnp.int32, (rows, rows // 2), 1)
        return jnp.where(r // 2 == c, 0.125, 0.0).astype(F32)

    for a in range(8):
        s = two_ref[2 * a] + two_ref[2 * a + 1]
        part_four[2 * a:2 * a + 1] = s[0:1] + s[1:2]
        part_four[2 * a + 1:2 * a + 2] = s[2:3] + s[3:4]
    four = jnp.dot(part_four[...], pool_matrix(256), precision=lax.Precision.HIGHEST, preferred_element_type=F32)
    for a in range(8):
        four_ref[a] = four[2 * a:2 * a + 2]
    rows = [four[4 * a:4 * a + 1] + four[4 * a + 1:4 * a + 2] + four[4 * a + 2:4 * a + 3] + four[4 * a + 3:4 * a + 4]
            for a in range(4)]
    eight = jnp.dot(jnp.concatenate(rows + rows, axis=0), pool_matrix(128),
                    precision=lax.Precision.HIGHEST, preferred_element_type=F32)
    for a in range(4):
        eight_ref[a] = eight[a:a + 1]

    for c in range(CHUNKS):
        for side in range(2):
            @pl.when(x_sides[side][0])
            def _():
                x_copy(side, c).wait_send()

            @pl.when(y_sides[side][0])
            def _():
                for t in range(2):
                    await_bytes(ue_s.at[t, side, c], se_s.at[t, side, c])
        near_copy(0, wyx0, c).wait_send()
        near_copy(1, wyx1, c).wait_send()
    for side in range(2):
        @pl.when(y_sides[side][0])
        def _():
            await_bytes(obse_s.at[side], se_s.at[2, side, 0])

    @pl.when(inner)
    def _():
        await_bytes(wb.at[0], sf_s.at[0])
        await_bytes(wb.at[1, 0], sf_s.at[1])
    for t in range(2):
        for way in range(2):
            await_bytes(wb.at[t, :, pl.ds(0, 15)], sa_s.at[t, way])
    await_bytes(obsb.at[:, pl.ds(0, 15)], so_s)
    await_bytes(sent_two.at[pl.ds(0, 15)], sp_s)


def shards(observed, profile_x, profile_y, profile_z):
    vmem = pl.BlockSpec(memory_space=pltpu.VMEM)
    smem = pl.BlockSpec(memory_space=pltpu.SMEM)
    dma = pltpu.SemaphoreType.DMA
    estimate, two, four, eight = pl.pallas_call(
        kernel,
        out_shape=[
            jax.ShapeDtypeStruct((1024, 128), F32),
            jax.ShapeDtypeStruct((16, 4, 256), F32),
            jax.ShapeDtypeStruct((8, 2, 128), F32),
            jax.ShapeDtypeStruct((4, 1, 64), F32),
        ],
        in_specs=[vmem, smem, smem, smem],
        out_specs=[vmem] * 4,
        scratch_shapes=[
            pltpu.VMEM((2, 256, 512), BF16),
            pltpu.VMEM((2, 256, 512), BF16),
            pltpu.VMEM((2, 2, 256, 256), BF16),
            pltpu.VMEM((2, 2, 256, 128), BF16),
            pltpu.VMEM((2, 128, 256), BF16),
            pltpu.VMEM((2, 128, 256), BF16),
            pltpu.VMEM((4, 16, 32, 128), F32),
            pltpu.VMEM((2, 16, 32, 128), F32),
            pltpu.VMEM((16, 32, 128), F32),
            pltpu.VMEM((2, 16, 8, 128), F32),
            pltpu.VMEM((2, 16, 8, 128), F32),
            pltpu.VMEM((2, 2, 16, 32, 128), F32),
            pltpu.VMEM((2, 2, 16, 32, 128), F32),
            pltpu.VMEM((2, 2, CHUNKS, 16, 8, 128), F32),
            pltpu.VMEM((2, 2, CHUNKS, 16, 8, 128), F32),
            pltpu.VMEM((3, 20, 32, 128), F32),
            pltpu.VMEM((3, 20, 32, 128), F32),
            pltpu.VMEM((2, 2, 16, 32, 128), F32),
            pltpu.VMEM((6, 16, 32, 128), F32),
            pltpu.VMEM((4, 16, 32, 128), F32),
            pltpu.VMEM((4, 16, 32, 128), F32),
            pltpu.VMEM((1024, 128), F32),
            pltpu.VMEM((512, 128), F32),
            pltpu.VMEM((2, 128, 128), F32),
            pltpu.VMEM((16, 8, 128), F32),
            pltpu.VMEM((16, 8, 128), F32),
            pltpu.VMEM((16, 256), F32),
            dma((2, CHUNKS)), dma((2, CHUNKS)),
            dma((2, CHUNKS)), dma((2, CHUNKS)),
            dma((2,)), dma((2, CHUNKS)),
            dma((3, 2, CHUNKS)), dma((3, 2, CHUNKS)),
            dma((2, 2)), dma((2, 2, CHUNKS)),
            dma, dma, dma, dma,
        ],
        compiler_params=pltpu.CompilerParams(
            collective_id=0, has_side_effects=True, vmem_limit_bytes=48 * 1024 * 1024),
        name="deconvolve",
    )(observed.reshape(1024, 128), profile_x, profile_y, profile_z)
    return estimate.reshape(32, 32, 128), two, four, eight


def solution(mesh):
    return jax.shard_map(
        shards,
        mesh=mesh,
        in_specs=(P("gz", "gx", "gy"), P(), P(), P()),
        out_specs=(
            P("gz", "gx", "gy"),
            P("gx", ("gy", "gz"), None),
            P("gx", ("gy", "gz"), None),
            P("gx", ("gy", "gz"), None),
        ),
        check_vma=False,
    )
```

time: 414 us -> 79.9 us (0.19)
  local copies, waits for them, and re-layouts: 113 us -> 4.3 us
  matrix products: 93.3 us -> 0 us
  waiting for transfers between devices: 80.1 us -> 0 us
  starting transfers between devices: 77.6 us -> 0 us
  Pallas kernels: 0 us -> 74.8 us
  other arithmetic: 25.7 us -> 0 us
  blocking collectives: 20.7 us -> 0 us
    dot_general x12 -> x0, matrix products: 93.3 us -> none  [the longest x4 84.2 us: along_y(): jnp.einsum('zxr,rc->zxc', extended, matrix, precision=lax.Precision.HIGHEST)]
    ppermute x24 -> x0, waiting for transfers between devices: 80.1 us -> none  [the longest x12 46.8 us: extended_2(): after = lax.ppermute(initial, axis, down)]
    ppermute x24 -> x0, starting transfers between devices: 77.6 us -> none  [the longest x12 59.1 us: extended_2(): before = lax.ppermute(last, axis, up)]
    pallas_call x0 -> x1, Pallas kernels: none -> 74.8 us  [shards(): pl.pallas_call(kernel, out_shape=[jax.ShapeDtypeStruct((1024, 128), F32),...]
    gather x10 -> x0, local copies, waits for them, and re-layouts: 60 us -> none  [band_matrix(): picked = kernel[jnp.clip(which, 0, tap_count - 1)]]
    reshape x1 -> x0, local copies, waits for them, and re-layouts: 34.8 us -> none  [pool_half(): field.reshape(sx // 2, 2, sy // 2, 2, sz // 2, 2).mean(axis=(1, 3, 5))]
    all_to_all x1 -> x0, blocking collectives: 20.7 us -> none  [shards(): lax.all_to_all(estimate, 'gz', split_axis=2, concat_axis=0, tiled=True)]
    reduce_sum x7 -> x0, other arithmetic: 18.6 us -> none  [the longest x4 14.9 us: pool_half(): field.reshape(sx // 2, 2, sy // 2, 2, sz // 2, 2).mean(axis=(1, 3, 5))]
  transfers between devices with their start and end apart: 24 -> 0, of which waited for: 16 -> 0; matrix products, arithmetic and copies ran while one was open for 16% -> 0% of each run, Pallas kernels for 0% -> 0%
where the time goes in v2:
time: 79.9 us; the launch traced here: 79.7 us
  Pallas kernels  74.8 us (94%)
  local copies, waits for them, and re-layouts  4.3 us (5%)
    pallas_call x1, Pallas kernels, shards(): pl.pallas_call(kernel, out_shape=[jax.ShapeDtypeStruct((1024, 128), F32),...  74.8 us
    unnamed x12, local copies, waits for them, and re-layouts  4.3 us

profile of v2, /device:TPU:1, one launch (start us, length us, event | category | flops | bytes accessed | tf_op | source)
XLA Modules:
  0.0 79.7 jit_solution(13426327060929184657)
XLA Ops:
  0.6 0.0 copy-start.3
  0.6 0.0 copy-start.2
  0.7 0.0 copy-start.1
  0.7 0.6 copy-done.3
  1.3 0.0 copy-done.2
  1.3 0.0 copy-done.1
  1.3 0.0 copy-start
  1.3 1.0 %copy-done = f32[32,32,128]{2,1,0:T(8,128)S(1)} copy-done((f32[32,32,128]{2,1,0:T(8,128)S(1)}, f32[32,32,128]{2,1,0:T(8,128)}, u32[]{:S(2)}) %copy-start) | copy-done | bytes 524312
  2.4 74.8 %deconvolve.1 = (f32[1024,128]{1,0:T(8,128)S(1)}, f32[16,4,256]{2,1,0:T(4,128)S(1)}, f32[8,2,128]{2,1,0:T(2,128)S(1)}, f32[4,1,64]{2,1,0:T(1,128)S(1)}) custom-call(f32[1024,128]{1,0:T(8,128)S(1)} %bitcast.2, f32[31]{0:T(128)S(1)} %copy-done.1, f32[31]{0:T(128)S(1)} %copy-done.2, f32[61]{0:T(128)S(1)} %copy-done.3), custom_call_target="tpu_custom_call" | custom-call | tf_op jit(solution)/shard_map/deconvolve/pallas_call | solution.py:428
  77.1 0.8 copy.12
  77.9 0.6 copy.13
  78.6 0.6 copy.14
  79.2 0.6 copy.15
Async XLA Ops:
  0.6 0.7 copy-start.3
  0.6 0.7 copy-start.2
  0.7 0.7 copy-start.1
  1.3 1.0 %copy-start = (f32[32,32,128]{2,1,0:T(8,128)S(1)}, f32[32,32,128]{2,1,0:T(8,128)}, u32[]{:S(2)}) copy-start(f32[32,32,128]{2,1,0:T(8,128)} %param.4) | copy-start | bytes 1572868

commit v3 on v2

--- a/solution.py
+++ b/solution.py
@@ -10,8 +10,8 @@
 MESH = pl.DeviceIdType.MESH
 F32, BF16 = jnp.float32, jnp.bfloat16
 CHUNKS = 2
-TILES = 4 // CHUNKS
 DEPTH = 32 // CHUNKS
+TILES = DEPTH // 8
 
 
 def split(value):
@@ -95,30 +95,39 @@
     return jnp.where(lane < width, left, right)
 
 
-def kernel(obs_ref, px, py, pz, est_ref, two_ref, four_ref, eight_ref,
-           xf, xa, yf, ya, zf, za, obsx, obsb, obss, obse_s, obse_r, u, um, ue_s, ue_r, zb, rb, wb,
-           wyx0, wyx1, est2, est3, pooled_z, pooled_t, sent_two, got_two, part_four,
+def kernel(obs_hbm, px, py, pz, est_ref, got_two,
+           obs_ref, obs_sem, xf, xa, yf, ya, zf, za, obsx, obsb, obss, obse_s, obse_r, u, um, ue_s, ue_r, zb, rb, wb,
+           wyx0, wyx1, est2, est3, pooled_z, pooled_t, sent_two,
            sx_s, sx_r, sn_s, sn_r, sf_s, sf_r, se_s, se_r, sa_s, sa_r, so_s, so_r, sp_s, sp_r):
     gx, gy, gz = lax.axis_index("gx"), lax.axis_index("gy"), lax.axis_index("gz")
     x_sides = ((gx > 0, {"gx": gx - 1}), (gx < 3, {"gx": gx + 1}))
     y_sides = ((gy > 0, gy - 1), (gy < 3, gy + 1))
     inner = (gx == 1) | (gx == 2)
+    outermost = ((gx == 1) & (gz == 0)) | ((gx == 2) & (gz == 15))
+    outer = ((gx == 1) & (gz < 2)) | ((gx == 2) & (gz > 13))
     parity = lax.rem(gx, 2)
 
-    obsx[0, 0] = jnp.zeros((32, 128), F32)
-    obsx[3, 15] = jnp.zeros((32, 128), F32)
+    load = pltpu.make_async_copy(obs_hbm, obs_ref, obs_sem)
+    load.start()
+
+    obsx[:, 0, 0] = jnp.zeros((CHUNKS, DEPTH, 128), F32)
+    obsx[:, 3, 15] = jnp.zeros((CHUNKS, DEPTH, 128), F32)
+    wyx0[:, 0:2, 0] = jnp.zeros((CHUNKS, 2, DEPTH, 128), F32)
+    wyx0[:, 14:16, 5] = jnp.zeros((CHUNKS, 2, DEPTH, 128), F32)
+    wyx1[:, 0, 0] = jnp.zeros((CHUNKS, DEPTH, 128), F32)
+    wyx1[:, 15, 3] = jnp.zeros((CHUNKS, DEPTH, 128), F32)
 
     @pl.when(gx == 0)
     def _():
-        obsx[0] = jnp.zeros((16, 32, 128), F32)
-        wyx0[0:2] = jnp.zeros((2, 16, 32, 128), F32)
-        wyx1[0] = jnp.zeros((16, 32, 128), F32)
+        obsx[:, 0] = jnp.zeros((CHUNKS, 16, DEPTH, 128), F32)
+        wyx0[:, :, 0:2] = jnp.zeros((CHUNKS, 16, 2, DEPTH, 128), F32)
+        wyx1[:, :, 0] = jnp.zeros((CHUNKS, 16, DEPTH, 128), F32)
 
     @pl.when(gx == 3)
     def _():
-        obsx[3] = jnp.zeros((16, 32, 128), F32)
-        wyx0[4:6] = jnp.zeros((2, 16, 32, 128), F32)
-        wyx1[3] = jnp.zeros((16, 32, 128), F32)
+        obsx[:, 3] = jnp.zeros((CHUNKS, 16, DEPTH, 128), F32)
+        wyx0[:, :, 4:6] = jnp.zeros((CHUNKS, 16, 2, DEPTH, 128), F32)
+        wyx1[:, :, 3] = jnp.zeros((CHUNKS, 16, DEPTH, 128), F32)
 
     for side in range(2):
         @pl.when(jnp.logical_not(y_sides[side][0]))
@@ -155,8 +164,11 @@
         def _():
             everyone(lambda d: greet({"gy": target, "gz": d}))
 
+    load.wait()
     for x in range(32):
-        obsx[1 + x // 16, x % 16] = obs_ref[pl.ds(x, 32, stride=32), :]
+        row = obs_ref[pl.ds(x, 32, stride=32), :]
+        for c in range(CHUNKS):
+            obsx[c, 1 + x // 16, x % 16] = row[DEPTH * c:DEPTH * c + DEPTH]
 
     neighbours = sum(there.astype(jnp.int32) for there, _ in y_sides) + inner.astype(jnp.int32)
     pl.semaphore_wait(barrier, 16 + 16 * neighbours)
@@ -164,12 +176,9 @@
     def await_bytes(ref, sem):
         pltpu.make_async_copy(ref, ref, sem).wait()
 
-    def z_of(c):
-        return pl.ds(DEPTH * c, DEPTH)
-
     def x_copy(side, c):
-        source = obsx.at[1, pl.ds(0, 15), z_of(c)] if side == 0 else obsx.at[2, pl.ds(1, 15), z_of(c)]
-        target = obsx.at[3, pl.ds(0, 15), z_of(c)] if side == 0 else obsx.at[0, pl.ds(1, 15), z_of(c)]
+        source = obsx.at[c, 1, pl.ds(0, 15)] if side == 0 else obsx.at[c, 2, pl.ds(1, 15)]
+        target = obsx.at[c, 3, pl.ds(0, 15)] if side == 0 else obsx.at[c, 0, pl.ds(1, 15)]
         return pltpu.make_async_remote_copy(
             src_ref=source, dst_ref=target, send_sem=sx_s.at[side, c], recv_sem=sx_r.at[side, c],
             device_id=x_sides[side][1], device_id_type=MESH)
@@ -185,10 +194,11 @@
             src_ref=source, dst_ref=target, send_sem=send_sem, recv_sem=recv_sem,
             device_id=device, device_id_type=MESH).start()
 
-    others(lambda d: send(obsx.at[pl.ds(1, 2), d], obsb.at[:, gz], so_s, so_r, {"gz": d}))
-    obsb[:, gz] = obsx[1:3, gz]
+    others(lambda d: send(obsx.at[:, pl.ds(1, 2), d], obsb.at[:, :, gz], so_s, so_r, {"gz": d}))
+    obsb[:, :, gz] = obsx[:, 1:3, gz]
     for side, first in ((0, 0), (1, 112)):
-        parts = [obsx[1 + j, :, 8 * k:8 * k + 8, :].reshape(128, 128) for k in range(4) for j in range(2)]
+        parts = [obsx[k // TILES, 1 + j, :, 8 * (k % TILES):8 * (k % TILES) + 8, :].reshape(128, 128)
+                 for k in range(4) for j in range(2)]
         obse_s[side] = gather_lanes(parts, 16, first).reshape(16, 8, 128)
 
         @pl.when(y_sides[side][0])
@@ -208,9 +218,12 @@
             ref[part, 18:20] = jnp.zeros((2, 32, 128), F32)
 
     def columns(ref, first, count, c):
-        parts = [ref[first:first + count, :, DEPTH * c + 8 * j:DEPTH * c + 8 * j + 8, :].reshape(128 * count, 128)
-                 for j in range(TILES)]
-        return parts[0] if TILES == 1 else jnp.concatenate(parts, axis=1)
+        parts = []
+        for k in range(TILES):
+            groups = [(ref[c, i, :, 8 * k:8 * k + 8, :] if ref.shape[1] < 16 else ref[c, :, i, 8 * k:8 * k + 8, :])
+                      .reshape(128, 128) for i in range(first, first + count)]
+            parts.append(jnp.concatenate(groups, axis=0))
+        return jnp.concatenate(parts, axis=1)
 
     def tile(value, j):
         return value[:, 128 * j:128 * j + 128]
@@ -218,16 +231,12 @@
     def blur_x(matrix, ref, first, c):
         return left_product(matrix, columns(ref, first, 4, c))
 
-    def store_columns(ref, first, value, c):
-        for j in range(TILES):
-            z = slice(DEPTH * c + 8 * j, DEPTH * c + 8 * j + 8)
-            ref[first:first + 2, :, z, :] = tile(value, j).reshape(2, 16, 8, 128)
-
     def to_columns(t, value, c):
-        store_columns(u.at[t], 0, value, c)
-        others(lambda d: send(u.at[t, :, d, z_of(c)], um.at[t, :, gz, z_of(c)], sa_s.at[t, 0], sa_r.at[t, 0, c],
-                              {"gz": d}))
         parts = [tile(value, k)[128 * j:128 * j + 128] for k in range(TILES) for j in range(2)]
+        for k in range(TILES):
+            for j in range(2):
+                u[t, c, :, j, 8 * k:8 * k + 8, :] = parts[2 * k + j].reshape(16, 8, 128)
+        others(lambda d: send(u.at[t, c, d], um.at[t, c, gz], sa_s.at[t, 0], sa_r.at[t, 0, c], {"gz": d}))
         for side, first in ((0, 0), (1, 96)):
             ue_s[t, side, c] = gather_lanes(parts, 32, first).reshape(16, 8, 128)
 
@@ -235,11 +244,12 @@
             def _():
                 everyone(lambda d: send(ue_s.at[t, side, c, d], ue_r.at[t, 1 - side, c, gz], se_s.at[t, side, c],
                                         se_r.at[t, 1 - side, c], {"gy": y_sides[side][1], "gz": d}))
-        um[t, :, gz, z_of(c), :] = u[t, :, gz, z_of(c), :]
+        um[t, c, gz] = u[t, c, gz]
 
     def middle(t, own):
         for c in range(CHUNKS):
-            await_bytes(um.at[t, :, pl.ds(0, 15), pl.ds(0, DEPTH)], sa_r.at[t, 0, c])
+            z = slice(DEPTH * c, DEPTH * c + DEPTH)
+            await_bytes(um.at[t, c, pl.ds(0, 15)], sa_r.at[t, 0, c])
             for side in range(2):
                 @pl.when(y_sides[side][0])
                 def _():
@@ -249,13 +259,13 @@
             for j in range(2):
                 halo = jnp.concatenate(
                     [spread_lanes(left, right, 32, 2 * k + j).reshape(16, 8, 128) for k in range(TILES)], axis=1)
-                own_lanes = um[t, j, :, DEPTH * c:DEPTH * c + DEPTH, :].reshape(16 * DEPTH, 128)
+                own_lanes = um[t, c, :, j].reshape(16 * DEPTH, 128)
                 result = right_product(jnp.concatenate([own_lanes, halo.reshape(16 * DEPTH, 128)], axis=1), yf.at[j])
-                zb[j, 2:18, DEPTH * c:DEPTH * c + DEPTH, :] = tile(result, 0).reshape(16, DEPTH, 128)
+                zb[j, 2:18, z, :] = tile(result, 0).reshape(16, DEPTH, 128)
                 sides = tile(result, 1) if sides is None else sides + tile(result, 1)
-            zb[2, 2:18, DEPTH * c:DEPTH * c + DEPTH, :] = sides.reshape(16, DEPTH, 128)
+            zb[2, 2:18, z, :] = sides.reshape(16, DEPTH, 128)
         if t == 0:
-            await_bytes(obsb.at[:, pl.ds(0, 15)], so_r)
+            await_bytes(obsb.at[:, :, pl.ds(0, 15)], so_r)
             for side in range(2):
                 @pl.when(y_sides[side][0])
                 def _():
@@ -271,42 +281,66 @@
             window = jnp.concatenate([zb[j, 4 * b:4 * b + 8].reshape(256, 128) for j in range(3)], axis=1)
             blurred = left_product(zf, window)
             for j in range(2):
-                ratio = obsb[j, 4 * b:4 * b + 4].reshape(128, 128) / tile(blurred, j)
+                seen = jnp.concatenate([obsb[c, j, 4 * b:4 * b + 4] for c in range(CHUNKS)], axis=1)
+                ratio = seen.reshape(128, 128) / tile(blurred, j)
                 rb[j, 2 + 4 * b:6 + 4 * b] = ratio.reshape(4, 32, 128)
             ratio = obss[4 * b:4 * b + 4].reshape(128, 128) / jnp.where(inside, tile(blurred, 2), 1.0)
             rb[2, 2 + 4 * b:6 + 4 * b] = jnp.where(inside, ratio, 0.0).reshape(4, 32, 128)
-        for b in range(4):
-            window = jnp.concatenate([rb[j, 4 * b:4 * b + 8].reshape(256, 128) for j in range(3)], axis=1)
+        def far(c, d):
+            target = {"gx": 3 - gx, "gz": d}
+            if t == 0:
+                first = 4 * (gx - 1)
+
+                @pl.when(jnp.logical_not(outer))
+                def _():
+                    send(wb.at[t, c, d], own.at[c, gz, pl.ds(first, 2)], sf_s.at[t], sf_r.at[t, c], target)
+
+                @pl.when(outer)
+                def _():
+                    send(wb.at[t, c, d, 2 - gx], own.at[c, gz, first + 2 - gx], sf_s.at[t], sf_r.at[t, c], target)
+            else:
+                @pl.when(jnp.logical_not(outermost))
+                def _():
+                    send(wb.at[t, c, d, 2 - gx], own.at[c, gz, 3 * (gx - 1)], sf_s.at[t], sf_r.at[t, c], target)
+
+        def near(c, d):
+            send(wb.at[t, c, d], own.at[c, gz, pl.ds(2 - t, 2)], sa_s.at[t, 1], sa_r.at[t, 1, c], {"gz": d})
+
+        for i in range(4):
+            b = lax.rem(gz // 4 + 1 + i, 4)
+            window = jnp.concatenate([rb[j, pl.ds(4 * b, 8)].reshape(256, 128) for j in range(3)], axis=1)
             back = left_product(za, window)
             for j in range(2):
                 result = right_product(jnp.concatenate([tile(back, j), tile(back, 2)], axis=1), ya.at[j])
-                wb[t, j, 4 * b:4 * b + 4] = result.reshape(4, 32, 128)
-        for c in range(CHUNKS):
+                result = result.reshape(4, 32, 128)
+                for c in range(CHUNKS):
+                    wb[t, c, pl.ds(4 * b, 4), j] = result[:, DEPTH * c:DEPTH * c + DEPTH]
+            for k in range(4):
+                d = 4 * b + lax.rem(gz + 1 + k, 4)
+
+                @pl.when(inner)
+                def _():
+                    far(0, d)
+                if i < 3 or k < 3:
+                    near(0, d)
+        for c in range(1, CHUNKS):
             @pl.when(inner)
             def _():
-                if t == 0:
-                    first = 4 * (gx - 1)
-                    everyone(lambda d: send(wb.at[t, :, d, z_of(c)], own.at[pl.ds(first, 2), gz, z_of(c)],
-                                            sf_s.at[t], sf_r.at[t, c], {"gx": 3 - gx, "gz": d}))
-                else:
-                    first = 3 * (gx - 1)
-                    everyone(lambda d: send(wb.at[t, 2 - gx, d, z_of(c)], own.at[first, gz, z_of(c)],
-                                            sf_s.at[t], sf_r.at[t, c], {"gx": 3 - gx, "gz": d}))
-            others(lambda d: send(wb.at[t, :, d, z_of(c)], own.at[pl.ds(2 - t, 2), gz, z_of(c)],
-                                  sa_s.at[t, 1], sa_r.at[t, 1, c], {"gz": d}))
-        own[2 - t:4 - t, gz] = wb[t, :, gz]
+                everyone(lambda d: far(c, d))
+            others(lambda d: near(c, d))
+        own[:, gz, 2 - t:4 - t] = wb[t, :, gz]
 
     def near_copy(t, ref, c):
         if t == 0:
-            source, target = ref.at[pl.ds(2, 2), :, z_of(c)], ref.at[pl.ds(4 * parity, 2), :, z_of(c)]
+            source, target = ref.at[c, :, pl.ds(2, 2)], ref.at[c, :, pl.ds(4 * parity, 2)]
         else:
-            source, target = ref.at[2 - parity, :, z_of(c)], ref.at[3 * parity, :, z_of(c)]
+            source, target = ref.at[c, :, 2 - parity], ref.at[c, :, 3 * parity]
         return pltpu.make_async_remote_copy(
             src_ref=source, dst_ref=target, send_sem=sn_s.at[t, c], recv_sem=sn_r.at[t, c],
             device_id={"gx": gx + 1 - 2 * parity}, device_id_type=MESH)
 
     def arrive_own(t, ref, c):
-        await_bytes(ref.at[pl.ds(2 - t, 2), pl.ds(0, 15), pl.ds(0, DEPTH)], sa_r.at[t, 1, c])
+        await_bytes(ref.at[c, pl.ds(0, 15), pl.ds(2 - t, 2)], sa_r.at[t, 1, c])
         near_copy(t, ref, c).start()
 
     def arrive_halos(t, ref, c):
@@ -314,7 +348,7 @@
 
         @pl.when(inner)
         def _():
-            await_bytes(ref.at[pl.ds(0, 2 - t), :, pl.ds(0, DEPTH)], sf_r.at[t, c])
+            await_bytes(ref.at[c, pl.ds(0, 15), pl.ds(0, 2 - t)], sf_r.at[t, c])
 
     for c in range(CHUNKS):
         for side in range(2):
@@ -330,7 +364,9 @@
         arrive_halos(0, wyx0, c)
         for half in range(2):
             correction = blur_x(xa, wyx0, 2 * half, c)
-            store_columns(est2, 2 * half, columns(obsx, 2 * half, 2, c) * correction, c)
+            new = columns(obsx, 2 * half, 2, c) * correction
+            for k in range(TILES):
+                est2[c, 2 * half:2 * half + 2, :, 8 * k:8 * k + 8, :] = tile(new, k).reshape(2, 16, 8, 128)
         to_columns(1, blur_x(xf, est2, 0, c), c)
     middle(1, wyx1)
 
@@ -339,9 +375,10 @@
     for c in range(CHUNKS):
         arrive_halos(1, wyx1, c)
         correction = blur_x(xa, wyx1, 0, c)
-        for j in range(TILES):
-            z = slice(DEPTH * c + 8 * j, DEPTH * c + 8 * j + 8)
-            new = est2[1:3, :, z, :].reshape(32, 8, 128) * tile(correction, j).reshape(32, 8, 128)
+        new_estimate = columns(est2, 1, 2, c) * correction
+        for k in range(TILES):
+            z = slice(DEPTH * c + 8 * k, DEPTH * c + 8 * k + 8)
+            new = tile(new_estimate, k).reshape(32, 8, 128)
             for x in range(32):
                 est3[32 * x + z.start:32 * x + z.stop] = new[x]
             for x in range(16):
@@ -359,6 +396,45 @@
     for z in range(32):
         est_ref[32 * z:32 * z + 32] = est3[pl.ds(z, 32, stride=32), :]
     await_bytes(got_two.at[pl.ds(0, 15)], sp_r)
+    for c in range(CHUNKS):
+        for side in range(2):
+            @pl.when(x_sides[side][0])
+            def _():
+                x_copy(side, c).wait_send()
+
+            @pl.when(y_sides[side][0])
+            def _():
+                for t in range(2):
+                    await_bytes(ue_s.at[t, side, c], se_s.at[t, side, c])
+        near_copy(0, wyx0, c).wait_send()
+        near_copy(1, wyx1, c).wait_send()
+    for side in range(2):
+        @pl.when(y_sides[side][0])
+        def _():
+            await_bytes(obse_s.at[side], se_s.at[2, side, 0])
+
+    @pl.when(inner & jnp.logical_not(outer))
+    def _():
+        await_bytes(wb.at[0], sf_s.at[0])
+
+    @pl.when(outer)
+    def _():
+        await_bytes(wb.at[0, :, :, 0], sf_s.at[0])
+
+    @pl.when(inner & jnp.logical_not(outermost))
+    def _():
+        await_bytes(wb.at[1, :, :, 0], sf_s.at[1])
+    for t in range(2):
+        for way in range(2):
+            await_bytes(wb.at[t, :, pl.ds(0, 15)], sa_s.at[t, way])
+    await_bytes(obsb.at[:, :, pl.ds(0, 15)], so_s)
+    await_bytes(sent_two.at[pl.ds(0, 15)], sp_s)
+
+
+def finish(est_in, got_two, est_out, two_out, four_out, eight_out, two_ref, four_ref, eight_ref, part_four, sems):
+    copies = [pltpu.make_async_copy(a, b, sems.at[i]) for i, (a, b) in enumerate(
+        ((est_in, est_out), (two_ref, two_out), (four_ref, four_out), (eight_ref, eight_out)))]
+    copies[0].start()
     group = lax.broadcasted_iota(jnp.int32, (8, 128), 1) // 16
     for half in range(2):
         blocks = [got_two[8 * half + s] for s in range(8)]
@@ -374,6 +450,8 @@
             two_ref[x, :, 128 * half:128 * half + 128] = blocks[x][0:4]
             two_ref[8 + x, :, 128 * half:128 * half + 128] = blocks[x][4:8]
 
+    copies[1].start()
+
     def pool_matrix(rows):
         r = lax.broadcasted_iota(jnp.int32, (rows, rows // 2), 0)
         c = lax.broadcasted_iota(jnp.int32, (rows, rows // 2), 1)
@@ -393,76 +471,49 @@
     for a in range(4):
         eight_ref[a] = eight[a:a + 1]
 
-    for c in range(CHUNKS):
-        for side in range(2):
-            @pl.when(x_sides[side][0])
-            def _():
-                x_copy(side, c).wait_send()
-
-            @pl.when(y_sides[side][0])
-            def _():
-                for t in range(2):
-                    await_bytes(ue_s.at[t, side, c], se_s.at[t, side, c])
-        near_copy(0, wyx0, c).wait_send()
-        near_copy(1, wyx1, c).wait_send()
-    for side in range(2):
-        @pl.when(y_sides[side][0])
-        def _():
-            await_bytes(obse_s.at[side], se_s.at[2, side, 0])
-
-    @pl.when(inner)
-    def _():
-        await_bytes(wb.at[0], sf_s.at[0])
-        await_bytes(wb.at[1, 0], sf_s.at[1])
-    for t in range(2):
-        for way in range(2):
-            await_bytes(wb.at[t, :, pl.ds(0, 15)], sa_s.at[t, way])
-    await_bytes(obsb.at[:, pl.ds(0, 15)], so_s)
-    await_bytes(sent_two.at[pl.ds(0, 15)], sp_s)
+    copies[2].start()
+    copies[3].start()
+    for copy in copies:
+        copy.wait()
 
 
 def shards(observed, profile_x, profile_y, profile_z):
     vmem = pl.BlockSpec(memory_space=pltpu.VMEM)
     smem = pl.BlockSpec(memory_space=pltpu.SMEM)
     dma = pltpu.SemaphoreType.DMA
-    estimate, two, four, eight = pl.pallas_call(
+    estimate, pieces = pl.pallas_call(
         kernel,
-        out_shape=[
-            jax.ShapeDtypeStruct((1024, 128), F32),
-            jax.ShapeDtypeStruct((16, 4, 256), F32),
-            jax.ShapeDtypeStruct((8, 2, 128), F32),
-            jax.ShapeDtypeStruct((4, 1, 64), F32),
-        ],
-        in_specs=[vmem, smem, smem, smem],
-        out_specs=[vmem] * 4,
+        out_shape=[jax.ShapeDtypeStruct((1024, 128), F32), jax.ShapeDtypeStruct((16, 8, 128), F32)],
+        in_specs=[pl.BlockSpec(memory_space=pltpu.HBM), smem, smem, smem],
+        out_specs=[vmem] * 2,
         scratch_shapes=[
+            pltpu.VMEM((1024, 128), F32),
+            dma,
             pltpu.VMEM((2, 256, 512), BF16),
             pltpu.VMEM((2, 256, 512), BF16),
             pltpu.VMEM((2, 2, 256, 256), BF16),
             pltpu.VMEM((2, 2, 256, 128), BF16),
             pltpu.VMEM((2, 128, 256), BF16),
             pltpu.VMEM((2, 128, 256), BF16),
-            pltpu.VMEM((4, 16, 32, 128), F32),
-            pltpu.VMEM((2, 16, 32, 128), F32),
+            pltpu.VMEM((CHUNKS, 4, 16, DEPTH, 128), F32),
+            pltpu.VMEM((CHUNKS, 2, 16, DEPTH, 128), F32),
             pltpu.VMEM((16, 32, 128), F32),
             pltpu.VMEM((2, 16, 8, 128), F32),
             pltpu.VMEM((2, 16, 8, 128), F32),
-            pltpu.VMEM((2, 2, 16, 32, 128), F32),
-            pltpu.VMEM((2, 2, 16, 32, 128), F32),
+            pltpu.VMEM((2, CHUNKS, 16, 2, DEPTH, 128), F32),
+            pltpu.VMEM((2, CHUNKS, 16, 2, DEPTH, 128), F32),
             pltpu.VMEM((2, 2, CHUNKS, 16, 8, 128), F32),
             pltpu.VMEM((2, 2, CHUNKS, 16, 8, 128), F32),
             pltpu.VMEM((3, 20, 32, 128), F32),
             pltpu.VMEM((3, 20, 32, 128), F32),
-            pltpu.VMEM((2, 2, 16, 32, 128), F32),
-            pltpu.VMEM((6, 16, 32, 128), F32),
-            pltpu.VMEM((4, 16, 32, 128), F32),
-            pltpu.VMEM((4, 16, 32, 128), F32),
+            pltpu.VMEM((2, CHUNKS, 16, 2, DEPTH, 128), F32),
+            pltpu.VMEM((CHUNKS, 16, 6, DEPTH, 128), F32),
+            pltpu.VMEM((CHUNKS, 16, 4, DEPTH, 128), F32),
+            pltpu.VMEM((CHUNKS, 4, 16, DEPTH, 128), F32),
             pltpu.VMEM((1024, 128), F32),
             pltpu.VMEM((512, 128), F32),
             pltpu.VMEM((2, 128, 128), F32),
             pltpu.VMEM((16, 8, 128), F32),
-            pltpu.VMEM((16, 8, 128), F32),
-            pltpu.VMEM((16, 256), F32),
             dma((2, CHUNKS)), dma((2, CHUNKS)),
             dma((2, CHUNKS)), dma((2, CHUNKS)),
             dma((2,)), dma((2, CHUNKS)),
@@ -474,6 +525,27 @@
             collective_id=0, has_side_effects=True, vmem_limit_bytes=48 * 1024 * 1024),
         name="deconvolve",
     )(observed.reshape(1024, 128), profile_x, profile_y, profile_z)
+    any_space = pl.BlockSpec(memory_space=pl.ANY)
+    estimate, two, four, eight = pl.pallas_call(
+        finish,
+        out_shape=[
+            jax.ShapeDtypeStruct((1024, 128), F32),
+            jax.ShapeDtypeStruct((16, 4, 256), F32),
+            jax.ShapeDtypeStruct((8, 2, 128), F32),
+            jax.ShapeDtypeStruct((4, 1, 64), F32),
+        ],
+        in_specs=[vmem] * 2,
+        out_specs=[any_space] * 4,
+        scratch_shapes=[
+            pltpu.VMEM((16, 4, 256), F32),
+            pltpu.VMEM((8, 2, 128), F32),
+            pltpu.VMEM((4, 1, 64), F32),
+            pltpu.VMEM((16, 256), F32),
+            dma((4,)),
+        ],
+        compiler_params=pltpu.CompilerParams(vmem_limit_bytes=16 * 1024 * 1024),
+        name="pyramid",
+    )(estimate, pieces)
     return estimate.reshape(32, 32, 128), two, four, eight
 
 

time: 79.9 us -> 76.4 us (0.956)
  local copies, waits for them, and re-layouts: 4.3 us -> 1.7 us
  Pallas kernels: 74.8 us -> 73.9 us
    unnamed x12 -> x8, local copies, waits for them, and re-layouts: 4.3 us -> 1.7 us
    pallas_call x1, Pallas kernels: 74.8 us -> 72.7 us  [shards(): pl.pallas_call(kernel, out_shape=[jax.ShapeDtypeStruct((1024, 128), F32),...]
    pallas_call x0 -> x1, Pallas kernels: none -> 1.25 us  [shards(): pl.pallas_call(finish, out_shape=[jax.ShapeDtypeStruct((1024, 128), F32),...]
where the time goes in v3:
time: 76.4 us; the launch traced here: 76.3 us
  Pallas kernels  73.9 us (97%)
  local copies, waits for them, and re-layouts  1.7 us (2%)
    pallas_call x1, Pallas kernels, shards(): pl.pallas_call(kernel, out_shape=[jax.ShapeDtypeStruct((1024, 128), F32),...  72.7 us
    unnamed x8, local copies, waits for them, and re-layouts  1.7 us

profile of v3, /device:TPU:1, one launch (start us, length us, event | category | flops | bytes accessed | tf_op | source)
XLA Modules:
  0.0 76.3 jit_solution(16697417995936923909)
XLA Ops:
  0.6 0.0 copy-start.3
  0.6 0.0 copy-start.2
  0.7 0.0 copy-start.1
  0.7 0.6 copy-done.3
  1.3 0.0 copy-done.2
  1.3 0.0 copy-done.1
  1.3 0.0 copy-start
  1.3 1.0 %copy-done = f32[32,32,128]{2,1,0:T(8,128)S(1)} copy-done((f32[32,32,128]{2,1,0:T(8,128)S(1)}, f32[32,32,128]{2,1,0:T(8,128)}, u32[]{:S(2)}) %copy-start) | copy-done | bytes 524312
  2.4 72.7 %deconvolve.1 = (f32[1024,128]{1,0:T(8,128)S(1)}, f32[16,8,128]{2,1,0:T(8,128)S(1)}) custom-call(f32[1024,128]{1,0:T(8,128)S(1)} %bitcast.2, f32[31]{0:T(128)S(1)} %copy-done.1, f32[31]{0:T(128)S(1)} %copy-done.2, f32[61]{0:T(128)S(1)} %copy-done.3), custom_call_target="tpu_custom_call" | custom-call | tf_op jit(solution)/shard_map/deconvolve/pallas_call | solution.py:484
  75.1 1.2 %pyramid.1 = (f32[1024,128]{1,0:T(8,128)}, f32[16,4,256]{2,1,0:T(4,128)}, f32[8,2,128]{2,1,0:T(2,128)}, f32[4,1,64]{2,1,0:T(1,128)}) custom-call(f32[1024,128]{1,0:T(8,128)S(1)} %get-tuple-element.10.est_in, f32[16,8,128]{2,1,0:T(8,128)S(1)} %get-tuple-element.11.got_two), custom_call_target="tpu_custom_call" | custom-call | tf_op jit(solution)/shard_map/pyramid/pallas_call | solution.py:529
Async XLA Ops:
  0.6 0.7 copy-start.3
  0.6 0.7 copy-start.2
  0.7 0.7 copy-start.1
  1.3 1.0 %copy-start = (f32[32,32,128]{2,1,0:T(8,128)S(1)}, f32[32,32,128]{2,1,0:T(8,128)}, u32[]{:S(2)}) copy-start(f32[32,32,128]{2,1,0:T(8,128)} %param.4) | copy-start | bytes 1572868

commit v4 on v3

--- a/solution.py
+++ b/solution.py
@@ -14,6 +14,9 @@
 TILES = DEPTH // 8
 
 
+SHIFTS = ((0, 0), (2, 2), (1, 2), (2, 1), (2, 3), (3, 2), (0, 2), (1, 1), (1, 3), (2, 0), (3, 1), (3, 3), (0, 1), (0, 3), (1, 0), (3, 0))
+
+
 def split(value):
     high = value.astype(BF16)
     return high, (value - high.astype(F32)).astype(BF16)
@@ -25,12 +28,16 @@
 
 def left_product(matrix, value):
     high, low = split(value)
-    return dot(matrix[0], high) + (dot(matrix[1], high) + dot(matrix[0], low))
+    rows = matrix.shape[0] // 2
+    both = dot(matrix[...], high)
+    return both[0:rows] + (both[rows:] + dot(matrix[0:rows], low))
 
 
 def right_product(value, matrix):
     high, low = split(value)
-    return dot(high, matrix[0]) + (dot(high, matrix[1]) + dot(low, matrix[0]))
+    rows = value.shape[0]
+    both = dot(jnp.concatenate([high, low], axis=0), matrix[0])
+    return both[0:rows] + (both[rows:] + dot(high, matrix[1]))
 
 
 def toeplitz(taps, count, rows, width, first, step):
@@ -47,9 +54,8 @@
 
 
 def store_split(ref, value):
-    high, low = split(value)
-    ref[0] = high
-    ref[1] = low
+    rows = value.shape[0]
+    ref[0:rows], ref[rows:] = split(value)
 
 
 def y_forward(ref, taps):
@@ -96,7 +102,7 @@
 
 
 def kernel(obs_hbm, px, py, pz, est_ref, got_two,
-           obs_ref, obs_sem, xf, xa, yf, ya, zf, za, obsx, obsb, obss, obse_s, obse_r, u, um, ue_s, ue_r, zb, rb, wb,
+           obs_ref, obs_sem, xf, xa, yf, ya, zf, za, obsx, obsb, obss, obse_s, obse_r, u, um, ue_s, ue_r, zb, ratios, rb, wb,
            wyx0, wyx1, est2, est3, pooled_z, pooled_t, sent_two,
            sx_s, sx_r, sn_s, sn_r, sf_s, sf_r, se_s, se_r, sa_s, sa_r, so_s, so_r, sp_s, sp_r):
     gx, gy, gz = lax.axis_index("gx"), lax.axis_index("gy"), lax.axis_index("gz")
@@ -141,17 +147,17 @@
     def greet(target):
         pl.semaphore_signal(barrier, inc=1, device_id=target, device_id_type=MESH)
 
+    def shifted(k, first):
+        a, b = SHIFTS[k + first]
+        return 4 * lax.rem(gz // 4 + a, 4) + lax.rem(gz + b, 4)
+
     def others(body):
-        def one(k, carry):
-            body(lax.rem(gz + k, 16))
-            return carry
-        lax.fori_loop(1, 16, one, 0)
+        for k in range(15):
+            body(shifted(k, 1))
 
     def everyone(body):
-        def one(k, carry):
-            body(lax.rem(gz + k, 16))
-            return carry
-        lax.fori_loop(0, 16, one, 0)
+        for k in range(16):
+            body(shifted(k, 0))
 
     greet({"gx": gx + 1 - 2 * parity})
 
@@ -212,8 +218,8 @@
     store_split(za, toeplitz(pz, 61, 128, 256, 94, -1))
     store_split(xa, toeplitz(px, 31, 256, 512, 248, -8))
     y_adjoint(ya, py)
-    for part in range(3):
-        for ref in (zb, rb):
+    for ref, parts in ((zb, 3), (rb, 2)):
+        for part in range(parts):
             ref[part, 0:2] = jnp.zeros((2, 32, 128), F32)
             ref[part, 18:20] = jnp.zeros((2, 32, 128), F32)
 
@@ -282,10 +288,13 @@
             blurred = left_product(zf, window)
             for j in range(2):
                 seen = jnp.concatenate([obsb[c, j, 4 * b:4 * b + 4] for c in range(CHUNKS)], axis=1)
-                ratio = seen.reshape(128, 128) / tile(blurred, j)
-                rb[j, 2 + 4 * b:6 + 4 * b] = ratio.reshape(4, 32, 128)
+                ratios[j, 128 * b:128 * b + 128] = seen.reshape(128, 128) / tile(blurred, j)
             ratio = obss[4 * b:4 * b + 4].reshape(128, 128) / jnp.where(inside, tile(blurred, 2), 1.0)
-            rb[2, 2 + 4 * b:6 + 4 * b] = jnp.where(inside, ratio, 0.0).reshape(4, 32, 128)
+            ratios[2, 128 * b:128 * b + 128] = jnp.where(inside, ratio, 0.0)
+        for j in range(2):
+            result = right_product(jnp.concatenate([ratios[j], ratios[2]], axis=1), ya.at[j])
+            rb[j, 2:18] = result.reshape(16, 32, 128)
+
         def far(c, d):
             target = {"gx": 3 - gx, "gz": d}
             if t == 0:
@@ -307,16 +316,15 @@
             send(wb.at[t, c, d], own.at[c, gz, pl.ds(2 - t, 2)], sa_s.at[t, 1], sa_r.at[t, 1, c], {"gz": d})
 
         for i in range(4):
-            b = lax.rem(gz // 4 + 1 + i, 4)
-            window = jnp.concatenate([rb[j, pl.ds(4 * b, 8)].reshape(256, 128) for j in range(3)], axis=1)
+            b = lax.rem(gz // 4 + (2, 1, 3, 0)[i], 4)
+            window = jnp.concatenate([rb[j, pl.ds(4 * b, 8)].reshape(256, 128) for j in range(2)], axis=1)
             back = left_product(za, window)
             for j in range(2):
-                result = right_product(jnp.concatenate([tile(back, j), tile(back, 2)], axis=1), ya.at[j])
-                result = result.reshape(4, 32, 128)
+                result = tile(back, j).reshape(4, 32, 128)
                 for c in range(CHUNKS):
                     wb[t, c, pl.ds(4 * b, 4), j] = result[:, DEPTH * c:DEPTH * c + DEPTH]
             for k in range(4):
-                d = 4 * b + lax.rem(gz + 1 + k, 4)
+                d = 4 * b + lax.rem(gz + (2, 1, 3, 0)[k], 4)
 
                 @pl.when(inner)
                 def _():
@@ -324,10 +332,11 @@
                 if i < 3 or k < 3:
                     near(0, d)
         for c in range(1, CHUNKS):
+            others(lambda d: near(c, d))
+
             @pl.when(inner)
             def _():
                 everyone(lambda d: far(c, d))
-            others(lambda d: near(c, d))
         own[:, gz, 2 - t:4 - t] = wb[t, :, gz]
 
     def near_copy(t, ref, c):
@@ -489,12 +498,12 @@
         scratch_shapes=[
             pltpu.VMEM((1024, 128), F32),
             dma,
-            pltpu.VMEM((2, 256, 512), BF16),
-            pltpu.VMEM((2, 256, 512), BF16),
+            pltpu.VMEM((512, 512), BF16),
+            pltpu.VMEM((512, 512), BF16),
             pltpu.VMEM((2, 2, 256, 256), BF16),
             pltpu.VMEM((2, 2, 256, 128), BF16),
-            pltpu.VMEM((2, 128, 256), BF16),
-            pltpu.VMEM((2, 128, 256), BF16),
+            pltpu.VMEM((256, 256), BF16),
+            pltpu.VMEM((256, 256), BF16),
             pltpu.VMEM((CHUNKS, 4, 16, DEPTH, 128), F32),
             pltpu.VMEM((CHUNKS, 2, 16, DEPTH, 128), F32),
             pltpu.VMEM((16, 32, 128), F32),
@@ -505,7 +514,8 @@
             pltpu.VMEM((2, 2, CHUNKS, 16, 8, 128), F32),
             pltpu.VMEM((2, 2, CHUNKS, 16, 8, 128), F32),
             pltpu.VMEM((3, 20, 32, 128), F32),
-            pltpu.VMEM((3, 20, 32, 128), F32),
+            pltpu.VMEM((3, 512, 128), F32),
+            pltpu.VMEM((2, 20, 32, 128), F32),
             pltpu.VMEM((2, CHUNKS, 16, 2, DEPTH, 128), F32),
             pltpu.VMEM((CHUNKS, 16, 6, DEPTH, 128), F32),
             pltpu.VMEM((CHUNKS, 16, 4, DEPTH, 128), F32),

time: 76.4 us -> 74.7 us (0.978)
  Pallas kernels: 73.9 us -> 71.5 us
    pallas_call x1, Pallas kernels: 72.7 us -> 70.3 us  [shards(): pl.pallas_call(kernel, out_shape=[jax.ShapeDtypeStruct((1024, 128), F32),...]
where the time goes in v4:
time: 74.7 us; the launch traced here: 73.9 us
  Pallas kernels  71.5 us (96%)
  local copies, waits for them, and re-layouts  1.7 us (2%)
    pallas_call x1, Pallas kernels, shards(): pl.pallas_call(kernel, out_shape=[jax.ShapeDtypeStruct((1024, 128), F32),...  70.3 us
    unnamed x8, local copies, waits for them, and re-layouts  1.7 us

profile of v4, /device:TPU:1, one launch (start us, length us, event | category | flops | bytes accessed | tf_op | source)
XLA Modules:
  0.0 73.9 jit_solution(8741539298744938275)
XLA Ops:
  0.6 0.0 copy-start.3
  0.6 0.0 copy-start.2
  0.7 0.0 copy-start.1
  0.7 0.6 copy-done.3
  1.3 0.0 copy-done.2
  1.3 0.0 copy-done.1
  1.3 0.0 copy-start
  1.3 1.0 %copy-done = f32[32,32,128]{2,1,0:T(8,128)S(1)} copy-done((f32[32,32,128]{2,1,0:T(8,128)S(1)}, f32[32,32,128]{2,1,0:T(8,128)}, u32[]{:S(2)}) %copy-start) | copy-done | bytes 524312
  2.4 70.3 %deconvolve.1 = (f32[1024,128]{1,0:T(8,128)S(1)}, f32[16,8,128]{2,1,0:T(8,128)S(1)}) custom-call(f32[1024,128]{1,0:T(8,128)S(1)} %bitcast.2, f32[31]{0:T(128)S(1)} %copy-done.1, f32[31]{0:T(128)S(1)} %copy-done.2, f32[61]{0:T(128)S(1)} %copy-done.3), custom_call_target="tpu_custom_call" | custom-call | tf_op jit(solution)/shard_map/deconvolve/pallas_call | solution.py:493
  72.6 1.2 %pyramid.1 = (f32[1024,128]{1,0:T(8,128)}, f32[16,4,256]{2,1,0:T(4,128)}, f32[8,2,128]{2,1,0:T(2,128)}, f32[4,1,64]{2,1,0:T(1,128)}) custom-call(f32[1024,128]{1,0:T(8,128)S(1)} %get-tuple-element.10.est_in, f32[16,8,128]{2,1,0:T(8,128)S(1)} %get-tuple-element.11.got_two), custom_call_target="tpu_custom_call" | custom-call | tf_op jit(solution)/shard_map/pyramid/pallas_call | solution.py:539
Async XLA Ops:
  0.6 0.7 copy-start.3
  0.6 0.7 copy-start.2
  0.7 0.7 copy-start.1
  1.3 1.0 %copy-start = (f32[32,32,128]{2,1,0:T(8,128)S(1)}, f32[32,32,128]{2,1,0:T(8,128)}, u32[]{:S(2)}) copy-start(f32[32,32,128]{2,1,0:T(8,128)} %param.4) | copy-start | bytes 1572868

commit v5 on v4

--- a/solution.py
+++ b/solution.py
@@ -14,7 +14,7 @@
 TILES = DEPTH // 8
 
 
-SHIFTS = ((0, 0), (2, 2), (1, 2), (2, 1), (2, 3), (3, 2), (0, 2), (1, 1), (1, 3), (2, 0), (3, 1), (3, 3), (0, 1), (0, 3), (1, 0), (3, 0))
+SHIFTS = ((0, 0), (2, 2), (2, 1), (2, 3), (2, 0), (1, 2), (3, 2), (1, 1), (1, 3), (3, 1), (3, 3), (1, 0), (3, 0), (0, 2), (0, 1), (0, 3))
 
 
 def split(value):
@@ -157,7 +157,7 @@
 
     def everyone(body):
         for k in range(16):
-            body(shifted(k, 0))
+            body(shifted((k + 1) % 16, 0))
 
     greet({"gx": gx + 1 - 2 * parity})
 

time: 74.7 us -> 74.3 us (level)
  no operation moved by 1% of the time
where the time goes in v5:
time: 74.3 us; the launch traced here: 73.2 us
  Pallas kernels  70.8 us (95%)
  local copies, waits for them, and re-layouts  1.7 us (2%)
    pallas_call x1, Pallas kernels, shards(): pl.pallas_call(kernel, out_shape=[jax.ShapeDtypeStruct((1024, 128), F32),...  69.6 us
    unnamed x8, local copies, waits for them, and re-layouts  1.7 us

profile of v5, /device:TPU:1, one launch (start us, length us, event | category | flops | bytes accessed | tf_op | source)
XLA Modules:
  0.0 73.2 jit_solution(2661849462025515707)
XLA Ops:
  0.6 0.0 copy-start.3
  0.6 0.0 copy-start.2
  0.7 0.0 copy-start.1
  0.7 0.6 copy-done.3
  1.3 0.0 copy-done.2
  1.3 0.0 copy-done.1
  1.3 0.0 copy-start
  1.3 1.0 %copy-done = f32[32,32,128]{2,1,0:T(8,128)S(1)} copy-done((f32[32,32,128]{2,1,0:T(8,128)S(1)}, f32[32,32,128]{2,1,0:T(8,128)}, u32[]{:S(2)}) %copy-start) | copy-done | bytes 524312
  2.4 69.6 %deconvolve.1 = (f32[1024,128]{1,0:T(8,128)S(1)}, f32[16,8,128]{2,1,0:T(8,128)S(1)}) custom-call(f32[1024,128]{1,0:T(8,128)S(1)} %bitcast.2, f32[31]{0:T(128)S(1)} %copy-done.1, f32[31]{0:T(128)S(1)} %copy-done.2, f32[61]{0:T(128)S(1)} %copy-done.3), custom_call_target="tpu_custom_call" | custom-call | tf_op jit(solution)/shard_map/deconvolve/pallas_call | solution.py:493
  72.0 1.2 %pyramid.1 = (f32[1024,128]{1,0:T(8,128)}, f32[16,4,256]{2,1,0:T(4,128)}, f32[8,2,128]{2,1,0:T(2,128)}, f32[4,1,64]{2,1,0:T(1,128)}) custom-call(f32[1024,128]{1,0:T(8,128)S(1)} %get-tuple-element.10.est_in, f32[16,8,128]{2,1,0:T(8,128)S(1)} %get-tuple-element.11.got_two), custom_call_target="tpu_custom_call" | custom-call | tf_op jit(solution)/shard_map/pyramid/pallas_call | solution.py:539
Async XLA Ops:
  0.6 0.7 copy-start.3
  0.6 0.7 copy-start.2
  0.7 0.7 copy-start.1
  1.3 1.0 %copy-start = (f32[32,32,128]{2,1,0:T(8,128)S(1)}, f32[32,32,128]{2,1,0:T(8,128)}, u32[]{:S(2)}) copy-start(f32[32,32,128]{2,1,0:T(8,128)} %param.4) | copy-start | bytes 1572868

commit v6 on v5

--- a/solution.py
+++ b/solution.py
@@ -113,7 +113,7 @@
     outer = ((gx == 1) & (gz < 2)) | ((gx == 2) & (gz > 13))
     parity = lax.rem(gx, 2)
 
-    load = pltpu.make_async_copy(obs_hbm, obs_ref, obs_sem)
+    load = pltpu.make_async_copy(obs_hbm, obs_ref.at[pl.ds(0, 1024)], obs_sem)
     load.start()
 
     obsx[:, 0, 0] = jnp.zeros((CHUNKS, DEPTH, 128), F32)
@@ -395,7 +395,7 @@
 
     halves = pooled_z[pl.ds(0, 256, stride=2), :] + pooled_z[pl.ds(1, 256, stride=2), :]
     for half in range(2):
-        pooled_t[half] = jnp.transpose(halves[128 * half:128 * half + 128])
+        pooled_t[half, 0:128] = jnp.transpose(halves[128 * half:128 * half + 128])
         even, odd = pooled_t[half, pl.ds(0, 64, stride=2), :], pooled_t[half, pl.ds(1, 64, stride=2), :]
         level = (even + odd) * 0.125
         for d in range(16):
@@ -496,7 +496,7 @@
         in_specs=[pl.BlockSpec(memory_space=pltpu.HBM), smem, smem, smem],
         out_specs=[vmem] * 2,
         scratch_shapes=[
-            pltpu.VMEM((1024, 128), F32),
+            pltpu.VMEM((1056, 128), F32),
             dma,
             pltpu.VMEM((512, 512), BF16),
             pltpu.VMEM((512, 512), BF16),
@@ -520,9 +520,9 @@
             pltpu.VMEM((CHUNKS, 16, 6, DEPTH, 128), F32),
             pltpu.VMEM((CHUNKS, 16, 4, DEPTH, 128), F32),
             pltpu.VMEM((CHUNKS, 4, 16, DEPTH, 128), F32),
-            pltpu.VMEM((1024, 128), F32),
-            pltpu.VMEM((512, 128), F32),
-            pltpu.VMEM((2, 128, 128), F32),
+            pltpu.VMEM((1056, 128), F32),
+            pltpu.VMEM((520, 128), F32),
+            pltpu.VMEM((2, 136, 128), F32),
             pltpu.VMEM((16, 8, 128), F32),
             dma((2, CHUNKS)), dma((2, CHUNKS)),
             dma((2, CHUNKS)), dma((2, CHUNKS)),

time: 74.3 us -> 74.3 us (level)
  no operation moved by 1% of the time
where the time goes in v6:
time: 74.3 us; the launch traced here: 73.2 us
  Pallas kernels  70.8 us (95%)
  local copies, waits for them, and re-layouts  1.7 us (2%)
    pallas_call x1, Pallas kernels, shards(): pl.pallas_call(kernel, out_shape=[jax.ShapeDtypeStruct((1024, 128), F32),...  69.6 us
    unnamed x8, local copies, waits for them, and re-layouts  1.7 us

profile of v6, /device:TPU:1, one launch (start us, length us, event | category | flops | bytes accessed | tf_op | source)
XLA Modules:
  0.0 73.2 jit_solution(13836684402113888809)
XLA Ops:
  0.6 0.0 copy-start.3
  0.6 0.0 copy-start.2
  0.7 0.0 copy-start.1
  0.7 0.6 copy-done.3
  1.3 0.0 copy-done.2
  1.3 0.0 copy-done.1
  1.3 0.0 copy-start
  1.3 1.0 %copy-done = f32[32,32,128]{2,1,0:T(8,128)S(1)} copy-done((f32[32,32,128]{2,1,0:T(8,128)S(1)}, f32[32,32,128]{2,1,0:T(8,128)}, u32[]{:S(2)}) %copy-start) | copy-done | bytes 524312
  2.4 69.6 %deconvolve.1 = (f32[1024,128]{1,0:T(8,128)S(1)}, f32[16,8,128]{2,1,0:T(8,128)S(1)}) custom-call(f32[1024,128]{1,0:T(8,128)S(1)} %bitcast.2, f32[31]{0:T(128)S(1)} %copy-done.1, f32[31]{0:T(128)S(1)} %copy-done.2, f32[61]{0:T(128)S(1)} %copy-done.3), custom_call_target="tpu_custom_call" | custom-call | tf_op jit(solution)/shard_map/deconvolve/pallas_call | solution.py:493
  71.9 1.2 %pyramid.1 = (f32[1024,128]{1,0:T(8,128)}, f32[16,4,256]{2,1,0:T(4,128)}, f32[8,2,128]{2,1,0:T(2,128)}, f32[4,1,64]{2,1,0:T(1,128)}) custom-call(f32[1024,128]{1,0:T(8,128)S(1)} %get-tuple-element.10.est_in, f32[16,8,128]{2,1,0:T(8,128)S(1)} %get-tuple-element.11.got_two), custom_call_target="tpu_custom_call" | custom-call | tf_op jit(solution)/shard_map/pyramid/pallas_call | solution.py:539
Async XLA Ops:
  0.6 0.7 copy-start.3
  0.6 0.7 copy-start.2
  0.7 0.7 copy-start.1
  1.3 1.0 %copy-start = (f32[32,32,128]{2,1,0:T(8,128)S(1)}, f32[32,32,128]{2,1,0:T(8,128)}, u32[]{:S(2)}) copy-start(f32[32,32,128]{2,1,0:T(8,128)} %param.4) | copy-start | bytes 1572868

commit v7 on v6

--- a/solution.py
+++ b/solution.py
@@ -254,6 +254,17 @@
 
     def middle(t, own):
         for c in range(CHUNKS):
+            if t == 0 and c == CHUNKS - 1:
+                await_bytes(obsb.at[:, :, pl.ds(0, 15)], so_r)
+                for side in range(2):
+                    @pl.when(y_sides[side][0])
+                    def _():
+                        await_bytes(obse_r.at[side], se_r.at[2, side, 0])
+                left, right = (obse_r[side].reshape(128, 128) for side in range(2))
+                lane = lax.broadcasted_iota(jnp.int32, (128, 128), 1)
+                for k in range(4):
+                    part = spread_lanes(left, right, 32, k)
+                    obss[:, 8 * k:8 * k + 8, :] = jnp.where(lane < 64, part, 0.0).reshape(16, 8, 128)
             z = slice(DEPTH * c, DEPTH * c + DEPTH)
             await_bytes(um.at[t, c, pl.ds(0, 15)], sa_r.at[t, 0, c])
             for side in range(2):
@@ -270,17 +281,6 @@
                 zb[j, 2:18, z, :] = tile(result, 0).reshape(16, DEPTH, 128)
                 sides = tile(result, 1) if sides is None else sides + tile(result, 1)
             zb[2, 2:18, z, :] = sides.reshape(16, DEPTH, 128)
-        if t == 0:
-            await_bytes(obsb.at[:, :, pl.ds(0, 15)], so_r)
-            for side in range(2):
-                @pl.when(y_sides[side][0])
-                def _():
-                    await_bytes(obse_r.at[side], se_r.at[2, side, 0])
-            left, right = (obse_r[side].reshape(128, 128) for side in range(2))
-            lane = lax.broadcasted_iota(jnp.int32, (128, 128), 1)
-            for k in range(4):
-                part = spread_lanes(left, right, 32, k)
-                obss[:, 8 * k:8 * k + 8, :] = jnp.where(lane < 64, part, 0.0).reshape(16, 8, 128)
         lane = lax.broadcasted_iota(jnp.int32, (128, 128), 1)
         inside = ((lane < 32) & (gy > 0)) | ((lane >= 32) & (lane < 64) & (gy < 3))
         for b in range(4):

time: 74.3 us -> 74.2 us (level)
  no operation moved by 1% of the time
where the time goes in v7:
time: 74.2 us; the launch traced here: 73.3 us
  Pallas kernels  70.9 us (96%)
  local copies, waits for them, and re-layouts  1.7 us (2%)
    pallas_call x1, Pallas kernels, shards(): pl.pallas_call(kernel, out_shape=[jax.ShapeDtypeStruct((1024, 128), F32),...  69.7 us
    unnamed x8, local copies, waits for them, and re-layouts  1.7 us

profile of v7, /device:TPU:1, one launch (start us, length us, event | category | flops | bytes accessed | tf_op | source)
XLA Modules:
  0.0 73.3 jit_solution(10361815099769294940)
XLA Ops:
  0.6 0.0 copy-start.3
  0.6 0.0 copy-start.2
  0.7 0.0 copy-start.1
  0.7 0.6 copy-done.3
  1.3 0.0 copy-done.2
  1.3 0.0 copy-done.1
  1.3 0.0 copy-start
  1.3 1.0 %copy-done = f32[32,32,128]{2,1,0:T(8,128)S(1)} copy-done((f32[32,32,128]{2,1,0:T(8,128)S(1)}, f32[32,32,128]{2,1,0:T(8,128)}, u32[]{:S(2)}) %copy-start) | copy-done | bytes 524312
  2.4 69.7 %deconvolve.1 = (f32[1024,128]{1,0:T(8,128)S(1)}, f32[16,8,128]{2,1,0:T(8,128)S(1)}) custom-call(f32[1024,128]{1,0:T(8,128)S(1)} %bitcast.2, f32[31]{0:T(128)S(1)} %copy-done.1, f32[31]{0:T(128)S(1)} %copy-done.2, f32[61]{0:T(128)S(1)} %copy-done.3), custom_call_target="tpu_custom_call" | custom-call | tf_op jit(solution)/shard_map/deconvolve/pallas_call | solution.py:493
  72.0 1.2 %pyramid.1 = (f32[1024,128]{1,0:T(8,128)}, f32[16,4,256]{2,1,0:T(4,128)}, f32[8,2,128]{2,1,0:T(2,128)}, f32[4,1,64]{2,1,0:T(1,128)}) custom-call(f32[1024,128]{1,0:T(8,128)S(1)} %get-tuple-element.10.est_in, f32[16,8,128]{2,1,0:T(8,128)S(1)} %get-tuple-element.11.got_two), custom_call_target="tpu_custom_call" | custom-call | tf_op jit(solution)/shard_map/pyramid/pallas_call | solution.py:539
Async XLA Ops:
  0.6 0.7 copy-start.3
  0.6 0.7 copy-start.2
  0.7 0.7 copy-start.1
  1.3 1.0 %copy-start = (f32[32,32,128]{2,1,0:T(8,128)S(1)}, f32[32,32,128]{2,1,0:T(8,128)}, u32[]{:S(2)}) copy-start(f32[32,32,128]{2,1,0:T(8,128)} %param.4) | copy-start | bytes 1572868
